TPU v7x, 256 devices: a whole 4x4x8 slice. The times are simulated.
256 devices in a mesh: freq: 8 (over x, z_lo), space: 32 (over z_hi, y, core).
Axes of the slice: x: 4, y: 4, z: 8 (z_hi: 4, z_lo: 2; z = z_hi * 2 + z_lo), core: 2. Of those that a mesh axis runs over, the one named last changes fastest.
Arguments:
- wavefield: float32 [8, 2, 2048, 4096], P('freq', None, 'space'), may hold values from -6 to 6
- velocity: float32 [8, 2048, 4096], P('freq', 'space'), may hold values from 1500 to 4500
- freq_index: int32 [8], P('freq'), may hold values from 0 to 63
- owner: int32 [8], replicated, may hold values from 0 to 7, each once
Outputs:
- image: float32 [2, 2048, 4096], P(None, 'space', 'freq')
- final_field: float32 [8, 2, 2048, 4096], P('freq', None, 'space')
Inputs may be any that keep to these rules, and one draw needn't show every extreme that they name: `owner`: each stored slice number appears once.
All inputs are finite; a program needn't handle non-finite values.
Results may differ from a plain program's by a relative error of at most 0.00022.
Values sent between devices are 32-bit elements; how exact they have to be, the bound alone decides.
A program may use at most 128 MiB of HBM per device.

v0:
```python
import math

import jax
import jax.numpy as jnp
from jax import lax
from jax.sharding import PartitionSpec as P

STEPS = 2


cell_spacing = 25.0
layer_thickness = 10.0
base_speed = 1500.0
lowest_hertz = 5.0
hertz_step = 0.9
highest = lax.Precision.HIGHEST


def from_root(value, axis, source):
    kept = jnp.where(lax.axis_index(axis) == source, value, 0).astype(value.dtype)
    return lax.psum(kept, axis)


def factor_pair(length):
    outer_len = 1
    for trial_size in range(1, length + 1):
        if trial_size * trial_size <= length and length % trial_size == 0:
            outer_len = trial_size
    return (outer_len, length // outer_len)


def dft_block(length, direction, factor):
    series = jnp.arange(length, dtype=jnp.int32)
    products = series[:, None] * series[None, :] % length
    angle = direction * 2 * math.pi / length * products.astype(jnp.float32)
    cosine = jnp.cos(angle) * factor
    sine = jnp.sin(angle) * factor
    upper = jnp.stack([cosine, sine], axis=1)
    lower = jnp.stack([-sine, cosine], axis=1)
    return jnp.stack([upper, lower], axis=0)


def twiddle_table(outer_len, inner_len, direction):
    total_len = outer_len * inner_len
    outer_idx = jnp.arange(outer_len, dtype=jnp.int32)
    inner_idx = jnp.arange(inner_len, dtype=jnp.int32)
    products = outer_idx[:, None] * inner_idx[None, :] % total_len
    angle = direction * 2 * math.pi / total_len * products.astype(jnp.float32)
    return (jnp.cos(angle), jnp.sin(angle))


def rotate(field, cos_part, sin_part):
    real_part = field[:, 0]
    imag_part = field[:, 1]
    return jnp.stack(
        [real_part * cos_part - imag_part * sin_part, real_part * sin_part + imag_part * cos_part],
        axis=1,
    )


def signed_wave(index, length):
    signed = jnp.where(index < length // 2, index, index - length)
    return signed.astype(jnp.float32) * (2 * math.pi / (length * cell_spacing))


def shards(wavefield, velocity, freq_index, owner):
    groups = lax.axis_size("space")
    column = lax.axis_index("space")
    count, _, rows_dev, width_x = wavefield.shape
    width_y = rows_dev * groups
    narrow = width_x // groups
    xa_len, xb_len = factor_pair(width_x)
    ya_len, yb_len = factor_pair(width_y)
    fwd_xa = dft_block(xa_len, -1.0, 1.0)
    fwd_xb = dft_block(xb_len, -1.0, 1.0)
    inv_xa = dft_block(xa_len, 1.0, 1.0 / xa_len)
    inv_xb = dft_block(xb_len, 1.0, 1.0 / xb_len)
    fwd_ya = dft_block(ya_len, -1.0, 1.0)
    fwd_yb = dft_block(yb_len, -1.0, 1.0)
    inv_ya = dft_block(ya_len, 1.0, 1.0 / ya_len)
    inv_yb = dft_block(yb_len, 1.0, 1.0 / yb_len)
    fx_cos, fx_sin = twiddle_table(xa_len, xb_len, -1.0)
    ix_cos, ix_sin = twiddle_table(xa_len, xb_len, 1.0)
    fy_cos, fy_sin = twiddle_table(ya_len, yb_len, -1.0)
    iy_cos, iy_sin = twiddle_table(ya_len, yb_len, 1.0)

    def forward_y(field):
        items = field.shape[4]
        shaped = field.reshape(count, 2, ya_len, yb_len, items)
        shaped = jnp.einsum("fcabw,caek->fekbw", shaped, fwd_ya, precision=highest)
        shaped = rotate(shaped, fy_cos[:, :, None], fy_sin[:, :, None])
        return jnp.einsum("fckbw,cbel->feklw", shaped, fwd_yb, precision=highest)

    def inverse_y(field):
        shaped = jnp.einsum("fcabw,cbel->fealw", field, inv_yb, precision=highest)
        shaped = rotate(shaped, iy_cos[:, :, None], iy_sin[:, :, None])
        shaped = jnp.einsum("fcabw,caek->fekbw", shaped, inv_ya, precision=highest)
        return shaped.reshape(count, 2, width_y, 1, narrow)

    omega = 2 * math.pi * (lowest_hertz + hertz_step * freq_index.astype(jnp.float32))
    position = column * narrow + jnp.arange(narrow, dtype=jnp.int32)
    kx_vals = signed_wave(position // xb_len + xa_len * (position % xb_len), width_x)
    ya_idx = jnp.arange(ya_len, dtype=jnp.int32)[:, None]
    yb_idx = jnp.arange(yb_len, dtype=jnp.int32)[None, :]
    ky_vals = signed_wave(ya_idx + ya_len * yb_idx, width_y)
    wave_sq = ky_vals[:, :, None] ** 2 + kx_vals[None, None, :] ** 2
    vertical = (omega[:, None, None, None] / base_speed) ** 2 - wave_sq[None]
    damping = jnp.exp(-layer_thickness * jnp.sqrt(jnp.maximum(-vertical, 0.0)))
    angle = layer_thickness * jnp.sqrt(jnp.maximum(vertical, 0.0))
    phase_cos = damping * jnp.cos(angle)
    phase_sin = damping * jnp.sin(angle)
    field = wavefield
    pieces = []
    for depth in range(STEPS):
        speed = from_root(velocity[0], "freq", owner[depth])
        forward_shaped = field.reshape(count, 2, rows_dev, xa_len, xb_len)
        forward_shaped = jnp.einsum("fcyab,caek->feykb", forward_shaped, fwd_xa, precision=highest)
        forward_shaped = rotate(forward_shaped, fx_cos, fx_sin)
        forward_shaped = jnp.einsum("fcykb,cbel->feykl", forward_shaped, fwd_xb, precision=highest)
        spectrum = forward_shaped.reshape(count, 2, rows_dev, groups, narrow)
        spectrum = lax.all_to_all(spectrum, "space", split_axis=3, concat_axis=2, tiled=True)
        spectrum = forward_y(spectrum)
        spectrum = rotate(spectrum, phase_cos, phase_sin)
        spectrum = inverse_y(spectrum)
        spectrum = lax.all_to_all(spectrum, "space", split_axis=2, concat_axis=3, tiled=True)
        inverse_shaped = spectrum.reshape(count, 2, rows_dev, xa_len, xb_len)
        inverse_shaped = jnp.einsum("fcyab,cbel->feyal", inverse_shaped, inv_xb, precision=highest)
        inverse_shaped = rotate(inverse_shaped, ix_cos, ix_sin)
        inverse_shaped = jnp.einsum("fcyab,caek->feykb", inverse_shaped, inv_xa, precision=highest)
        field = inverse_shaped.reshape(count, 2, rows_dev, width_x)
        slowness = 1.0 / speed - 1.0 / base_speed
        shift = omega[:, None, None] * layer_thickness * slowness[None]
        field = rotate(field, jnp.cos(shift), jnp.sin(shift))
        term = jnp.sum(field[:, 0], axis=0)
        pieces.append(lax.psum_scatter(term, "freq", scatter_dimension=1, tiled=True))
    image = jnp.stack(pieces, axis=0)
    return (image, field)


def solution(mesh):
    return jax.shard_map(
        shards,
        mesh=mesh,
        in_specs=(P("freq", None, "space", None), P("freq", "space", None), P("freq"), P()),
        out_specs=(P(None, "space", "freq"), P("freq", None, "space", None)),
        check_vma=False,
    )
```

profile of v0, /device:TPU:8, one launch (start us, length us, event | category | flops | bytes accessed | tf_op | source)
XLA Modules:
  0.0 551.9 jit_solution(8522332523889777303)
XLA Ops:
  7.6 4.6 reshape.775
  12.3 5.5 fusion.16
  17.8 1.0 multiply_subtract_fusion.3
  18.8 7.6 %fusion.19 = f32[1,2,64,64,64]{3,4,2,1,0:T(8,128)} fusion(f32[1,64,2,64]{1,3,0,2:T(8,128)S(1)} %get-tuple-element.33, f32[1,64,2,64]{1,3,0,2:T(8,128)S(1)} %get-tuple-element.32, f32[1,1,64,64,64]{4,3,2,1,0:T(8,128)S(1)} %get-tuple-element.11, f32[1,1,64,64,64]{4,3,2,1,0:T(8,128)S(1)} %get-tuple-element.10), kind=kOutput, calls=%fused_computation.22 | convolution fusion | flops 805847040 | bytes 4259840 | tf_op jit(solution)/shard_map/fcykb,cbel->feykl/dot_general | solution.py:119
  26.4 5.7 %copy.107 = f32[1,2,64,64,64]{4,3,2,1,0:T(8,128)} copy(f32[1,2,64,64,64]{3,4,2,1,0:T(8,128)} %fusion.19) | data formatting | bytes 4194304 | tf_op jit(solution)/shard_map/fcykb,cbel->feykl/transpose | solution.py:119
  32.1 3.3 reshape.777
  35.4 2.9 copy.108
  38.3 12.0 %all-to-all-start = ((f32[1,2,64,32,128]{4,1,2,0,3:T(2,128)}), f32[1,2,64,32,128]{4,1,2,0,3:T(2,128)S(1)}, u32[]{:S(2)}, u32[]{:S(2)}) async-start(f32[1,2,64,32,128]{4,1,2,0,3:T(2,128)} %copy.108), calls=%async_computation | async-start | bytes 4194304 | tf_op jit(solution)/shard_map/all_to_all | solution.py:121
  52.2 49.0 %all-to-all-done = f32[1,2,64,32,128]{4,1,2,0,3:T(2,128)S(1)} async-done(((f32[1,2,64,32,128]{4,1,2,0,3:T(2,128)}), f32[1,2,64,32,128]{4,1,2,0,3:T(2,128)S(1)}, u32[]{:S(2)}, u32[]{:S(2)}) %all-to-all-start) | async-done | bytes 2097184 | tf_op jit(solution)/shard_map/all_to_all | solution.py:121
  101.2 3.1 fusion.74
  104.3 0.7 multiply_subtract_fusion.11
  105.0 0.2 maximum_bitcast_fusion.8
  105.2 3.0 fusion.56
  108.2 5.0 multiply_subtract_fusion.10
  113.3 2.0 fusion.59
  115.3 0.9 multiply_subtract_fusion.9
  116.2 0.2 maximum_bitcast_fusion.10
  116.4 3.1 fusion.62
  119.5 1.2 copy.117
  120.7 8.6 %copy.118 = f32[1,2,2048,1,128]{4,1,3,0,2:T(2,128)} copy(f32[1,2,2048,1,128]{4,2,1,3,0:T(8,128)S(1)} %bitcast.323) | data formatting | bytes 4194304 | tf_op jit(solution)/shard_map/reshape;fcabw,caek->fekbw/transpose | solution.py:98
  129.3 5.6 %all-to-all-start.1 = ((f32[1,2,2048,1,128]{4,1,3,0,2:T(2,128)}), f32[1,2,2048,1,128]{4,1,3,0,2:T(2,128)S(1)}, u32[]{:S(2)}, u32[]{:S(2)}) async-start(f32[1,2,2048,1,128]{4,1,3,0,2:T(2,128)} %copy.118), calls=%async_computation.1 | async-start | bytes 4194304 | tf_op jit(solution)/shard_map/all_to_all | solution.py:125
  135.0 1.3 fusion.132
  137.6 1.5 select_bitcast_fusion
  139.6 60.1 %all-to-all-done.1 = f32[1,2,2048,1,128]{4,1,3,0,2:T(2,128)S(1)} async-done(((f32[1,2,2048,1,128]{4,1,3,0,2:T(2,128)}), f32[1,2,2048,1,128]{4,1,3,0,2:T(2,128)S(1)}, u32[]{:S(2)}, u32[]{:S(2)}) %all-to-all-start.1) | async-done | bytes 2097184 | tf_op jit(solution)/shard_map/all_to_all | solution.py:125
  199.8 1.2 copy.120
  201.0 2.8 reshape.812
  203.8 8.0 %convolution_bitcast_fusion.1 = f32[1,2,64,64,64]{3,4,2,1,0:T(8,128)S(1)} fusion(f32[2,64,64,64,1]{3,2,0,1,4:T(8,128)} %reshape.812, f32[1,64,2,64]{1,3,2,0:T(8,128)S(1)} %get-tuple-element.31, f32[1,64,2,64]{1,3,2,0:T(8,128)S(1)} %get-tuple-element.30), kind=kOutput, calls=%fused_computation.28 | convolution fusion | flops 805322752 | bytes 4259840 | tf_op jit(solution)/shard_map/fcyab,cbel->feyal/dot_general | solution.py:127
  211.8 1.0 multiply_subtract_fusion.2
  212.8 7.6 %fusion.22 = f32[1,2,64,64,64]{4,3,2,1,0:T(8,128)} fusion(f32[1,1,64,64,64]{3,4,2,1,0:T(8,128)S(1)} %get-tuple-element.9, f32[1,1,64,64,64]{3,4,2,1,0:T(8,128)S(1)} %get-tuple-element.8, f32[1,64,2,64]{1,3,2,0:T(8,128)S(1)} %get-tuple-element.31, f32[1,64,2,64]{1,3,2,0:T(8,128)S(1)} %get-tuple-element.30), kind=kOutput, calls=%fused_computation.23 | convolution fusion | flops 805847040 | bytes 4259840 | tf_op jit(solution)/shard_map/fcyab,caek->feykb/dot_general | solution.py:129
  220.4 3.5 reshape.784
  224.0 55.1 %all-reduce.3.cloned.1.call-done = (f32[64,4096]{1,0:T(8,128)}, f32[64,4096]{1,0:T(8,128)}) async-done(((f32[64,4096]{1,0:T(8,128)}, f32[64,4096]{1,0:T(8,128)}), (f32[64,4096]{1,0:T(8,128)}, f32[64,4096]{1,0:T(8,128)})) %all-reduce.3.cloned.1.call-update) | async-done | bytes 2097168 | tf_op jit(solution)/shard_map/psum | solution.py:21
  279.1 5.7 %multiply_subtract_fusion.8 = (f32[64,4096]{1,0:T(8,128)S(1)}, f32[64,4096]{1,0:T(8,128)}) fusion(f32[1,2,64,4096]{3,2,1,0:T(8,128)S(1)} %reshape.784, f32[64,4096]{1,0:T(8,128)} %get-tuple-element.2, f32[]{:T(128)} %bitcast.72), kind=kLoop, calls=%fused_computation.91 | loop fusion | flops 2359296 | bytes 5242884 | tf_op jit(solution)/shard_map/sub | solution.py:56
  284.8 2.5 stack.105
  287.3 2.2 stack.104
  289.5 5.4 fusion.31
  294.9 1.0 multiply_subtract_fusion.1
  295.9 7.7 %fusion.25 = f32[1,2,64,64,64]{3,4,2,1,0:T(8,128)} fusion(f32[1,64,2,64]{1,3,0,2:T(8,128)S(1)} %get-tuple-element.33, f32[1,64,2,64]{1,3,0,2:T(8,128)S(1)} %get-tuple-element.32, f32[1,1,64,64,64]{4,3,2,1,0:T(8,128)S(1)} %get-tuple-element.7, f32[1,1,64,64,64]{4,3,2,1,0:T(8,128)S(1)} %get-tuple-element.6), kind=kOutput, calls=%fused_computation.24 | convolution fusion | flops 805847040 | bytes 4259840 | tf_op jit(solution)/shard_map/fcykb,cbel->feykl/dot_general | solution.py:119
  303.6 5.7 %copy.127 = f32[1,2,64,64,64]{4,3,2,1,0:T(8,128)} copy(f32[1,2,64,64,64]{3,4,2,1,0:T(8,128)} %fusion.25) | data formatting | bytes 4194304 | tf_op jit(solution)/shard_map/fcykb,cbel->feykl/transpose | solution.py:119
  309.3 3.3 reshape.787
  312.5 1.6 copy.128
  314.2 59.6 %all_to_all.60 = f32[1,2,64,32,128]{4,1,2,0,3:T(2,128)S(1)} all-to-all(f32[1,2,64,32,128]{4,1,2,0,3:T(2,128)S(1)} %copy.128), channel_id=1, replica_groups=mesh['freq'=8,'space'=32] {'space'}, dimensions={3} | all-to-all | bytes 4194304 | tf_op jit(solution)/shard_map/all_to_all | solution.py:121
  373.8 3.1 fusion.77
  376.9 0.7 multiply_subtract_fusion.7
  377.8 3.0 fusion.65
  380.9 5.0 multiply_subtract_fusion.6
  385.9 2.0 fusion.68
  387.9 1.1 multiply_subtract_fusion.5
  389.0 0.2 maximum_bitcast_fusion.13
  389.3 3.1 fusion.71
  392.3 1.2 copy.135
  393.6 8.6 %copy.136 = f32[1,2,2048,1,128]{4,1,3,0,2:T(2,128)} copy(f32[1,2,2048,1,128]{4,2,1,3,0:T(8,128)S(1)} %bitcast.325) | data formatting | bytes 4194304 | tf_op jit(solution)/shard_map/reshape;fcabw,caek->fekbw/transpose | solution.py:98
  402.1 6.4 %all-to-all-start.3 = ((f32[1,2,2048,1,128]{4,1,3,0,2:T(2,128)}), f32[1,2,2048,1,128]{4,1,3,0,2:T(2,128)S(1)}, u32[]{:S(2)}, u32[]{:S(2)}) async-start(f32[1,2,2048,1,128]{4,1,3,0,2:T(2,128)} %copy.136), calls=%async_computation.4 | async-start | bytes 4194304 | tf_op jit(solution)/shard_map/all_to_all | solution.py:125
  408.6 0.7 reduce-scatter.3.cloned.1.call-update
  409.3 64.0 %all-to-all-done.3 = f32[1,2,2048,1,128]{4,1,3,0,2:T(2,128)S(1)} async-done(((f32[1,2,2048,1,128]{4,1,3,0,2:T(2,128)}), f32[1,2,2048,1,128]{4,1,3,0,2:T(2,128)S(1)}, u32[]{:S(2)}, u32[]{:S(2)}) %all-to-all-start.3) | async-done | bytes 2097184 | tf_op jit(solution)/shard_map/all_to_all | solution.py:125
  473.5 1.2 copy.138
  474.7 2.5 reshape.832
  477.3 8.0 %convolution_bitcast_fusion = f32[1,2,64,64,64]{3,4,2,1,0:T(8,128)S(1)} fusion(f32[2,64,64,64,1]{3,2,0,1,4:T(8,128)} %reshape.832, f32[1,64,2,64]{1,3,2,0:T(8,128)S(1)} %get-tuple-element.31, f32[1,64,2,64]{1,3,2,0:T(8,128)S(1)} %get-tuple-element.30), kind=kOutput, calls=%fused_computation.27 | convolution fusion | flops 805322752 | bytes 4259840 | tf_op jit(solution)/shard_map/fcyab,cbel->feyal/dot_general | solution.py:127
  485.3 1.0 multiply_subtract_fusion
  486.2 7.6 %fusion.28 = f32[1,2,64,64,64]{4,3,2,1,0:T(8,128)} fusion(f32[1,1,64,64,64]{3,4,2,1,0:T(8,128)S(1)} %get-tuple-element.5, f32[1,1,64,64,64]{3,4,2,1,0:T(8,128)S(1)} %get-tuple-element.4, f32[1,64,2,64]{1,3,2,0:T(8,128)S(1)} %get-tuple-element.31, f32[1,64,2,64]{1,3,2,0:T(8,128)S(1)} %get-tuple-element.30), kind=kOutput, calls=%fused_computation.25 | convolution fusion | flops 805847040 | bytes 4259840 | tf_op jit(solution)/shard_map/fcyab,caek->feykb/dot_general | solution.py:129
  493.9 3.5 reshape.794
  497.4 5.7 %add_bitcast_fusion = (f32[1,1,64,4096]{3,2,1,0:T(8,128)S(1)}, f32[64,4096]{1,0:T(8,128)}) fusion(f32[1,2,64,4096]{3,2,1,0:T(8,128)S(1)} %reshape.794, f32[64,4096]{1,0:T(8,128)} %get-tuple-element.3, f32[]{:T(128)} %bitcast.72), kind=kLoop, calls=%fused_computation.80 | loop fusion | flops 2359296 | bytes 5242884 | tf_op jit(solution)/shard_map/stack | solution.py:55
  503.1 2.7 pad_maximum_fusion
  505.8 37.6 %reduce-scatter.5.cloned.1.call-done = f32[64,512]{1,0:T(8,128)} async-done(((f32[64,4096]{1,0:T(8,128)}), f32[64,512]{1,0:T(8,128)}) %reduce-scatter.5.cloned.1.call-update) | async-done | bytes 131088 | tf_op jit(solution)/shard_map/reduce_scatter | solution.py:135
  543.4 1.7 pad_maximum_fusion.1
  (74 shorter events, 2.7 us)
Async XLA Ops:
  7.6 10.2 %copy-start.2 = (f32[64,64]{1,0:T(8,128)}, f32[64,64]{1,0:T(8,128)S(1)}, u32[]{:S(2)}) copy-start(f32[64,64]{1,0:T(8,128)S(1)} %get-tuple-element.42) | copy-start | bytes 49156
  7.6 10.2 %copy-start.4 = (f32[64,64]{1,0:T(8,128)}, f32[64,64]{1,0:T(8,128)S(1)}, u32[]{:S(2)}) copy-start(f32[64,64]{1,0:T(8,128)S(1)} %get-tuple-element.43) | copy-start | bytes 49156
  38.3 62.9 %all-to-all-start = ((f32[1,2,64,32,128]{4,1,2,0,3:T(2,128)}), f32[1,2,64,32,128]{4,1,2,0,3:T(2,128)S(1)}, u32[]{:S(2)}, u32[]{:S(2)}) async-start(f32[1,2,64,32,128]{4,1,2,0,3:T(2,128)} %copy.108), calls=%async_computation | async-start | bytes 4194304 | tf_op jit(solution)/shard_map/all_to_all | solution.py:121
  51.1 53.1 %copy-start.6 = (f32[32,64]{0,1:T(8,128)}, f32[32,64]{0,1:T(8,128)S(1)}, u32[]{:S(2)}) copy-start(f32[32,64]{0,1:T(8,128)S(1)} %copy.110) | copy-start | bytes 24580
  51.3 53.0 %copy-start.8 = (f32[32,64]{0,1:T(8,128)}, f32[32,64]{0,1:T(8,128)S(1)}, u32[]{:S(2)}) copy-start(f32[32,64]{0,1:T(8,128)S(1)} %copy.111) | copy-start | bytes 24580
  51.3 56.9 %copy-start.18 = (f32[128]{0:T(128)}, f32[128]{0:T(128)S(1)}, u32[]{:S(2)}) copy-start(f32[128]{0:T(128)S(1)} %fusion.123) | copy-start | bytes 1540
  51.9 63.4 %copy-start.14 = (f32[32,64]{1,0:T(8,128)}, f32[32,64]{1,0:T(8,128)S(1)}, u32[]{:S(2)}) copy-start(f32[32,64]{1,0:T(8,128)S(1)} %get-tuple-element.49) | copy-start | bytes 24580
  52.2 56.0 %copy-start.16 = (f32[32,64]{1,0:T(8,128)}, f32[32,64]{1,0:T(8,128)S(1)}, u32[]{:S(2)}) copy-start(f32[32,64]{1,0:T(8,128)S(1)} %fusion.108) | copy-start | bytes 24580
  129.3 8.3 %copy-start.1 = (f32[1,64,4096]{2,1,0:T(8,128)S(1)}, f32[1,64,4096]{2,1,0:T(8,128)}, u32[]{:S(2)}) copy-start(f32[1,64,4096]{2,1,0:T(8,128)} %param.5) | copy-start | bytes 3145732
  129.3 70.4 %all-to-all-start.1 = ((f32[1,2,2048,1,128]{4,1,3,0,2:T(2,128)}), f32[1,2,2048,1,128]{4,1,3,0,2:T(2,128)S(1)}, u32[]{:S(2)}, u32[]{:S(2)}) async-start(f32[1,2,2048,1,128]{4,1,3,0,2:T(2,128)} %copy.118), calls=%async_computation.1 | async-start | bytes 4194304 | tf_op jit(solution)/shard_map/all_to_all | solution.py:125
  134.9 144.2 %all-reduce.3.cloned.1.call-start = ((), (), s32[]{:S(2)}) async-start(), calls=%async_computation.8 | async-start | bytes 4194304 | tf_op jit(solution)/shard_map/psum | solution.py:21
  139.3 72.4 %copy-start.10 = (f32[64,64]{0,1:T(8,128)}, f32[64,64]{0,1:T(8,128)S(1)}, u32[]{:S(2)}) copy-start(f32[64,64]{0,1:T(8,128)S(1)} %copy.122) | copy-start | bytes 49156
  139.6 72.2 %copy-start.12 = (f32[64,64]{0,1:T(8,128)}, f32[64,64]{0,1:T(8,128)S(1)}, u32[]{:S(2)}) copy-start(f32[64,64]{0,1:T(8,128)S(1)} %copy.123) | copy-start | bytes 49156
  284.8 4.7 copy-start
  289.5 5.4 copy-start.3
  289.5 5.4 copy-start.5
  373.8 3.1 copy-start.7
  373.8 3.1 copy-start.9
  377.8 3.0 copy-start.17
  377.8 3.0 copy-start.19
  385.9 2.0 copy-start.15
  402.1 71.3 %all-to-all-start.3 = ((f32[1,2,2048,1,128]{4,1,3,0,2:T(2,128)}), f32[1,2,2048,1,128]{4,1,3,0,2:T(2,128)S(1)}, u32[]{:S(2)}, u32[]{:S(2)}) async-start(f32[1,2,2048,1,128]{4,1,3,0,2:T(2,128)} %copy.136), calls=%async_computation.4 | async-start | bytes 4194304 | tf_op jit(solution)/shard_map/all_to_all | solution.py:125
  408.5 97.3 %reduce-scatter.3.cloned.1.call-start = ((), (), s32[]{:S(2)}) async-start(), calls=%async_computation.6 | async-start | bytes 1179648 | tf_op jit(solution)/shard_map/reduce_scatter | solution.py:135
  409.3 134.2 %reduce-scatter.5.cloned.1.call-start = ((), (), s32[]{:S(2)}) async-start(), calls=%async_computation.7 | async-start | bytes 1179648 | tf_op jit(solution)/shard_map/reduce_scatter | solution.py:135
  477.2 8.0 %copy-start.11 = (f32[64,64]{0,1:T(8,128)S(1)}, f32[64,64]{0,1:T(8,128)}, u32[]{:S(2)}) copy-start(f32[64,64]{0,1:T(8,128)} %copy-done.10) | copy-start | bytes 49156
  477.2 8.0 %copy-start.13 = (f32[64,64]{0,1:T(8,128)S(1)}, f32[64,64]{0,1:T(8,128)}, u32[]{:S(2)}) copy-start(f32[64,64]{0,1:T(8,128)} %copy-done.12) | copy-start | bytes 49156
Sparse Core Ops, SparseCore 0:
  139.2 139.7 all-reduce.2
  411.9 66.9 reduce-scatter.2
  503.2 40.1 reduce-scatter.4
where the time goes:
time: 560 us; the launch traced here: 552 us
  waiting for transfers between devices  267 us (48%)
  matrix products  79.7 us (14%)
  local copies, waits for them, and re-layouts  68.1 us (12%)
  blocking collectives  59.6 us (11%)
  other arithmetic  37.2 us (7%)
  starting transfers between devices  24.1 us (4%)
  between operations  16.5 us (3%)
    all_to_all x2, waiting for transfers between devices, shards(): lax.all_to_all(spectrum, 'space', split_axis=2, concat_axis=3, tiled=True)  124 us
    all_to_all x1, blocking collectives, shards(): lax.all_to_all(spectrum, 'space', split_axis=3, concat_axis=2, tiled=True)  59.6 us
    psum x1, waiting for transfers between devices, from_root(): return lax.psum(kept, axis)  55.1 us
    all_to_all x1, waiting for transfers between devices, shards(): lax.all_to_all(spectrum, 'space', split_axis=3, concat_axis=2, tiled=True)  49 us
    reduce_scatter x2, waiting for transfers between devices, shards(): lax.psum_scatter(term, 'freq', scatter_dimension=1, tiled=True)  37.6 us
    sub x11, other arithmetic, rotate(): real_part * cos_part - imag_part * sin_part  23.1 us
    transpose x2, local copies, waits for them, and re-layouts, inverse_y(): return shaped.reshape(count, 2, width_y, 1, narrow)  17.1 us
    dot_general x2, matrix products, shards(): jnp.einsum('fcyab,cbel->feyal', inverse_shaped, inv_xb, precision=highest)  16 us
  transfers between devices with their start and end apart: 6, of which 5 were waited for; matrix products, arithmetic and copies ran while one was open for 11% of the time, Pallas kernels for 0%

commit v1 on v0

v1 whole, which is shorter than its diff:
```python
import functools
import math

import jax
import jax.numpy as jnp
import ml_dtypes
import numpy as np
from jax import lax
from jax.experimental import pallas as pl
from jax.experimental.pallas import tpu as pltpu
from jax.sharding import PartitionSpec as P

NX, NY = 4096, 2048
SPACE, FREQ = 32, 8
ROWS = NY // SPACE
LANES = 128
TILES = NX // LANES
YA = NY // LANES
CHUNK = 32
CHUNKS = ROWS // CHUNK
BAND = NX // FREQ
PIECE = ROWS // FREQ

cell_spacing = 25.0
layer_thickness = 10.0
base_speed = 1500.0
lowest_hertz = 5.0
hertz_step = 0.9
MESH = pl.DeviceIdType.MESH
f32 = jnp.float32
bf16 = jnp.bfloat16


def times_root(value, power, length, sign):
    re, im = value
    power = power % length
    quarter = 4 * power
    if quarter % length == 0:
        turn = quarter // length
        if sign < 0:
            turn = (4 - turn) % 4
        return [(re, im), (-im, re), (-re, -im), (im, -re)][turn]
    angle = sign * 2 * math.pi * power / length
    c, s = math.cos(angle), math.sin(angle)
    if (8 * power) % length == 0:
        h = math.sqrt(0.5)
        cs, ss = math.copysign(1, c), math.copysign(1, s)
        p, q = re * h, im * h
        real = (p if cs > 0 else -p) + (-q if ss > 0 else q)
        imag = (p if ss > 0 else -p) + (q if cs > 0 else -q)
        return (real, imag)
    return (re * c - im * s, re * s + im * c)


def add(a, b):
    return (a[0] + b[0], a[1] + b[1])


def sub(a, b):
    return (a[0] - b[0], a[1] - b[1])


def small_dft(values, sign):
    n = len(values)
    if n == 1:
        return values
    if n == 2:
        return [add(values[0], values[1]), sub(values[0], values[1])]
    m = n // 4
    parts = [small_dft(values[r::4], sign) for r in range(4)]
    out = [None] * n
    for k in range(m):
        a = parts[0][k]
        b, c, d = (times_root(parts[r][k], r * k, n, sign) for r in (1, 2, 3))
        s0, s1 = add(a, c), sub(a, c)
        s2, s3 = add(b, d), times_root(sub(b, d), 1, 4, sign)
        out[k], out[k + m] = add(s0, s2), add(s1, s3)
        out[k + 2 * m], out[k + 3 * m] = sub(s0, s2), sub(s1, s3)
    return out


def sin_cos(t):
    n = jnp.floor(t * (2 / math.pi) + 0.5)
    r = (t - n * 1.5703125) - n * 4.83826794896e-4
    z = r * r
    s = r + r * z * (-1.6666654611e-1 + z * (8.3321608736e-3 + z * -1.9515295891e-4))
    c = 1.0 - 0.5 * z + z * z * (4.166664568298827e-2 + z * (-1.388731625493765e-3 + z * 2.443315711809948e-5))
    half = n * 0.5
    odd = half != jnp.floor(half)
    quad = n - 4.0 * jnp.floor(n * 0.25)
    sine = jnp.where(odd, c, s)
    cosine = jnp.where(odd, s, c)
    sine = jnp.where(quad >= 2.0, -sine, sine)
    cosine = jnp.where((quad == 1.0) | (quad == 2.0), -cosine, cosine)
    return sine, cosine


def split(value):
    high = value.astype(bf16)
    return high, (value - high.astype(f32)).astype(bf16)


def mul3(a, b):
    ah, al = a
    bh, bl = b
    dot = functools.partial(jnp.dot, preferred_element_type=f32)
    return dot(ah, bh) + (dot(al, bh) + dot(ah, bl))


def kernel(
    fidx_ref, owner_ref, wave_ref, vel_ref, txc_ref, txs_ref, rh_ref, rl_ref, lh_ref, ll_ref,
    image_ref, field_ref,
    rowbuf, sendx, sendy, recvy, recvx, mid, hcos, hsin, tyc, tys,
    vrecv, vsel, slow, phc, phs, terms, imag, irecv,
    asend, arecv, aloc, vsend, vrcv, vloc, gsend, grecv, isend, ircv, iloc,
):
    f = lax.axis_index("freq")
    me = lax.axis_index("space")
    zh, yy, cc = me // 8, (me // 2) % 4, me % 2

    def space_peer(j):
        return ((zh + j // 8) % 4 * 4 + (yy + (j // 2) % 4) % 4) * 2 + (cc + j % 2) % 2

    def freq_peer(j):
        return (f + j) % FREQ

    barrier = pltpu.get_barrier_semaphore()

    @pl.loop(1, SPACE)
    def _(j):
        pl.semaphore_signal(barrier, inc=1, device_id=(f, space_peer(j)), device_id_type=MESH)

    @pl.loop(1, FREQ)
    def _(j):
        pl.semaphore_signal(barrier, inc=1, device_id=(freq_peer(j), me), device_id_type=MESH)

    pl.semaphore_wait(barrier, SPACE + FREQ - 2)

    def remote(src, dst, send, recv, device):
        return pltpu.make_async_remote_copy(
            src_ref=src, dst_ref=dst, send_sem=send, recv_sem=recv, device_id=device, device_id_type=MESH
        )

    def a2a_start(src, dst, ch, i):
        rows = pl.ds(ch * CHUNK, CHUNK)

        @pl.loop(1, SPACE)
        def _(j):
            d = space_peer(j)
            remote(src.at[d, rows], dst.at[me, rows], asend.at[i, ch], arecv.at[i, ch], (f, d)).start()

        pltpu.make_async_copy(src.at[me, rows], dst.at[me, rows], aloc.at[i, ch]).start()

    def a2a_all(src, dst, ch, i):
        rows = pl.ds(ch * CHUNK, CHUNK)
        some = pl.ds(0, SPACE - 1)
        return remote(src.at[some, rows], dst.at[some, rows], asend.at[i, ch], arecv.at[i, ch], (f, me))

    def a2a_wait_recv(src, dst, ch, i):
        rows = pl.ds(ch * CHUNK, CHUNK)
        a2a_all(src, dst, ch, i).wait_recv()
        pltpu.make_async_copy(src.at[me, rows], dst.at[me, rows], aloc.at[i, ch]).wait()

    def forward_x(re_ref, im_ref, dst, ch):
        @pl.loop(0, CHUNK // 8)
        def _(g):
            rows = pl.ds(pl.multiple_of(ch * CHUNK + g * 8, 8), 8)
            local = pl.ds(pl.multiple_of(g * 8, 8), 8)
            vals = [
                (re_ref[rows, a * LANES:(a + 1) * LANES], im_ref[rows, a * LANES:(a + 1) * LANES])
                for a in range(TILES)
            ]
            vals = small_dft(vals, -1)
            for k in range(TILES):
                re, im = vals[k]
                c, s = txc_ref[k:k + 1, :], txs_ref[k:k + 1, :]
                rowbuf[k, local, 0:LANES] = re * c + im * s
                rowbuf[k, local, LANES:] = im * c - re * s

        @pl.loop(0, TILES // 8)
        def _(g):
            some = pl.ds(g * 8, 8)
            block = rowbuf[some].reshape(8 * CHUNK, 2 * LANES)
            out = mul3(split(block), (rh_ref[...], rl_ref[...]))
            dst[some, pl.ds(ch * CHUNK, CHUNK), :] = out.reshape(8, CHUNK, 2 * LANES)

    def inverse_x(src, step, re_ref, im_ref, ch):
        @pl.loop(0, TILES // 8)
        def _(g):
            some = pl.ds(g * 8, 8)
            block = src[some, pl.ds(ch * CHUNK, CHUNK), :].reshape(8 * CHUNK, 2 * LANES)
            out = mul3(split(block), (lh_ref[...], ll_ref[...]))
            rowbuf[some] = out.reshape(8, CHUNK, 2 * LANES)

        @pl.loop(0, CHUNK // 8)
        def _(g):
            rows = pl.ds(pl.multiple_of(ch * CHUNK + g * 8, 8), 8)
            local = pl.ds(pl.multiple_of(g * 8, 8), 8)
            vals = []
            for k in range(TILES):
                re, im = rowbuf[k, local, 0:LANES], rowbuf[k, local, LANES:]
                c, s = txc_ref[k:k + 1, :], txs_ref[k:k + 1, :]
                vals.append((re * c - im * s, im * c + re * s))
            vals = small_dft(vals, 1)
            for a in range(TILES):
                re, im = vals[a]
                cols = slice(a * LANES, (a + 1) * LANES)
                c, s = phc[step, rows, cols], phs[step, rows, cols]
                re_ref[rows, cols] = re * c - im * s
                im_ref[rows, cols] = re * s + im * c

    def column_pass(src, dst, i):
        @pl.loop(0, LANES // 8)
        def _(t):
            half, sub_rows = t // 8, pl.ds(pl.multiple_of(t % 8 * 8, 8), 8)
            vals = [
                (src[2 * a + half, sub_rows, 0:LANES], src[2 * a + half, sub_rows, LANES:]) for a in range(YA)
            ]
            vals = small_dft(vals, -1)
            re_rows = pl.ds(pl.multiple_of(t * 8, 8), 8)
            im_rows = pl.ds(pl.multiple_of(LANES + t * 8, 8), 8)
            for k in range(YA):
                re, im = vals[k]
                cols = slice(k % 2 * LANES, k % 2 * LANES + LANES)
                c, s = tyc[k // 2, re_rows, cols], tys[k // 2, re_rows, cols]
                mid[k // 2, re_rows, cols] = re * c + im * s
                mid[k // 2, im_rows, cols] = im * c - re * s

        @pl.loop(0, YA // 2)
        def _(k):
            left = (lh_ref[...], ll_ref[...])
            spec = mul3(left, split(mid[k]))
            re, im = spec[:LANES], spec[LANES:]
            c, s = hcos[k], hsin[k]
            spec = jnp.concatenate([re * c - im * s, re * s + im * c], axis=0)
            mid[k] = mul3((rh_ref[...], rl_ref[...]), split(spec))

        for ch in range(CHUNKS):
            @pl.loop(0, CHUNK // 4)
            def _(q):
                half, tile = q % 2, ch * (CHUNK // 8) + q // 2
                t = half * 8 + tile
                re_rows = pl.ds(pl.multiple_of(t * 8, 8), 8)
                im_rows = pl.ds(pl.multiple_of(LANES + t * 8, 8), 8)
                vals = []
                for k in range(YA):
                    cols = slice(k % 2 * LANES, k % 2 * LANES + LANES)
                    re, im = mid[k // 2, re_rows, cols], mid[k // 2, im_rows, cols]
                    c, s = tyc[k // 2, re_rows, cols], tys[k // 2, re_rows, cols]
                    vals.append((re * c - im * s, im * c + re * s))
                vals = small_dft(vals, 1)
                out_rows = pl.ds(pl.multiple_of(tile * 8, 8), 8)
                for a in range(YA):
                    dst[2 * a + half, out_rows, 0:LANES] = vals[a][0]
                    dst[2 * a + half, out_rows, LANES:] = vals[a][1]
            a2a_start(dst, recvx.at[i // 2], ch, i)

    omega = 2 * math.pi * (lowest_hertz + hertz_step * fidx_ref[0].astype(f32))

    def make_tables():
        kb = lax.broadcasted_iota(jnp.int32, (LANES, LANES), 0)
        lane = lax.broadcasted_iota(jnp.int32, (LANES, LANES), 1)
        jx = me + TILES * lane
        kx = jnp.where(jx < NX // 2, jx, jx - NX).astype(f32) * (2 * math.pi / (NX * cell_spacing))

        @pl.loop(0, YA // 2)
        def _(k):
            for part in range(2):
                ka = 2 * k + part
                cols = slice(part * LANES, (part + 1) * LANES)
                jy = ka + YA * kb
                ky = jnp.where(jy < NY // 2, jy, jy - NY).astype(f32) * (2 * math.pi / (NY * cell_spacing))
                vertical = (omega / base_speed) ** 2 - (ky * ky + kx * kx)
                root = layer_thickness * jnp.sqrt(jnp.abs(vertical))
                damping = jnp.exp(jnp.where(vertical < 0.0, -root, 0.0)) * (1.0 / (NX * NY))
                sine, cosine = sin_cos(jnp.where(vertical > 0.0, root, 0.0))
                hcos[k, :, cols] = damping * cosine
                hsin[k, :, cols] = damping * sine
                sine, cosine = sin_cos((ka * kb).astype(f32) * (2 * math.pi / NY))
                tyc[k, :, cols] = cosine
                tys[k, :, cols] = sine

    def make_phase(step):
        @pl.loop(0, ROWS // 8)
        def _(g):
            rows = pl.ds(pl.multiple_of(g * 8, 8), 8)
            for q in range(4):
                cols = slice(q * NX // 4, (q + 1) * NX // 4)
                shift = (omega * layer_thickness) * slow[step, rows, cols]
                sine, cosine = sin_cos(shift)
                phc[step, rows, cols] = cosine
                phs[step, rows, cols] = sine

    def vel_all(sem):
        return remote(vrecv.at[pl.ds(0, FREQ - 1)], vrecv.at[pl.ds(0, FREQ - 1)], vsend.at[0], sem, (f, me))

    def gather_all(step):
        part = slow.at[step, pl.ds(0, (FREQ - 1) * PIECE)]
        return remote(part, part, gsend.at[step], grecv.at[step], (f, me))

    mine8 = pl.ds(pl.multiple_of(f * PIECE, PIECE), PIECE)

    def velocity_start():
        @pl.loop(1, FREQ)
        def _(j):
            p = freq_peer(j)
            rows = pl.ds(pl.multiple_of(p * PIECE, PIECE), PIECE)
            remote(vel_ref.at[rows], vrecv.at[f], vsend.at[0], vrcv.at[0], (p, me)).start()
        pltpu.make_async_copy(vel_ref.at[mine8], vrecv.at[f], vloc.at[0]).start()

    def velocity_share():
        vel_all(vrcv.at[0]).wait_recv()
        pltpu.make_async_copy(vel_ref.at[mine8], vrecv.at[f], vloc.at[0]).wait()
        for step in range(2):
            piece = 1.0 / vrecv[owner_ref[step]] - 1.0 / base_speed
            vsel[step] = piece
            slow[step, mine8] = piece

            @pl.loop(1, FREQ)
            def _(j):
                remote(vsel.at[step], slow.at[step, mine8], gsend.at[step], grecv.at[step], (freq_peer(j), me)).start()

    def image_start(step, ch):
        rows = pl.ds(ch * CHUNK, CHUNK)

        @pl.loop(1, FREQ)
        def _(j):
            p = freq_peer(j)
            cols = pl.ds(pl.multiple_of(p * BAND, BAND), BAND)
            remote(
                terms.at[step, rows, cols], irecv.at[step, f, rows],
                isend.at[step, ch], ircv.at[step, ch], (p, me),
            ).start()

        cols = pl.ds(pl.multiple_of(f * BAND, BAND), BAND)
        pltpu.make_async_copy(terms.at[step, rows, cols], irecv.at[step, f, rows], iloc.at[step, ch]).start()

    def image_all(step, ch):
        part = irecv.at[step, pl.ds(0, FREQ - 1), pl.ds(ch * CHUNK, CHUNK)]
        return remote(part, part, isend.at[step, ch], ircv.at[step, ch], (f, me))

    def image_finish(step, ch):
        rows = pl.ds(ch * CHUNK, CHUNK)
        image_all(step, ch).wait_recv()
        part = irecv.at[step, 0, rows]
        pltpu.make_async_copy(part, part, iloc.at[step, ch]).wait()
        total = irecv[step, 0, rows, :]
        for j in range(1, FREQ):
            total = total + irecv[step, j, rows, :]
        image_ref[step, rows, :] = total

    velocity_start()
    for ch in range(CHUNKS):
        forward_x(wave_ref.at[0, 0], wave_ref.at[0, 1], sendx.at[0], ch)
        a2a_start(sendx.at[0], recvy.at[0], ch, 0)
    make_tables()
    velocity_share()
    gather_all(0).wait_recv()
    gather_all(1).wait_recv()
    make_phase(0)
    make_phase(1)
    for ch in range(CHUNKS):
        a2a_wait_recv(sendx.at[0], recvy.at[0], ch, 0)
    column_pass(recvy.at[0], sendy.at[0], 1)
    for ch in range(CHUNKS):
        a2a_wait_recv(sendy.at[0], recvx.at[0], ch, 1)
        inverse_x(recvx.at[0], 0, terms.at[0], imag, ch)
        forward_x(terms.at[0], imag, sendx.at[1], ch)
        a2a_start(sendx.at[1], recvy.at[1], ch, 2)
        image_start(0, ch)
    for ch in range(CHUNKS):
        a2a_wait_recv(sendx.at[1], recvy.at[1], ch, 2)
    column_pass(recvy.at[1], sendy.at[1], 3)
    for ch in range(CHUNKS):
        image_finish(0, ch)
    for ch in range(CHUNKS):
        a2a_wait_recv(sendy.at[1], recvx.at[1], ch, 3)
        inverse_x(recvx.at[1], 1, terms.at[1], field_ref.at[0, 1], ch)
        image_start(1, ch)
        rows = slice(ch * CHUNK, (ch + 1) * CHUNK)
        field_ref[0, 0, rows, :] = terms[1, rows, :]
    for ch in range(CHUNKS):
        image_finish(1, ch)

    vel_all(vrcv.at[0]).wait_send()
    for step in range(2):
        remote(slow.at[step, pl.ds(0, (FREQ - 1) * PIECE)], slow.at[step, pl.ds(0, (FREQ - 1) * PIECE)], gsend.at[step], grecv.at[step], (f, me)).wait_send()
    for ch in range(CHUNKS):
        for i in range(4):
            src = (sendx if i % 2 == 0 else sendy).at[i // 2]
            a2a_all(src, src, ch, i).wait_send()
        for step in range(2):
            image_all(step, ch).wait_send()


def tables():
    n = np.arange(LANES)
    angle = 2 * np.pi * ((n[:, None] * n[None, :]) % LANES) / LANES
    c, s = np.cos(angle), np.sin(angle)
    right = np.block([[c, -s], [s, c]])
    out = []
    for m in (right, right.T):
        high = m.astype(ml_dtypes.bfloat16)
        out += [high, (m - high.astype(np.float64)).astype(ml_dtypes.bfloat16)]
    tx = 2 * np.pi * ((np.arange(TILES)[:, None] * n[None, :]) % NX) / NX
    return [np.cos(tx).astype(np.float32), np.sin(tx).astype(np.float32)] + out


def shards(wavefield, velocity, freq_index, owner):
    vmem = pl.BlockSpec(memory_space=pltpu.VMEM)
    smem = pl.BlockSpec(memory_space=pltpu.SMEM)
    dma = pltpu.SemaphoreType.DMA
    big = (SPACE, ROWS, 2 * LANES)
    image, field = pl.pallas_call(
        kernel,
        out_shape=(
            jax.ShapeDtypeStruct((2, ROWS, BAND), f32),
            jax.ShapeDtypeStruct((1, 2, ROWS, NX), f32),
        ),
        in_specs=[smem, smem] + [vmem] * 8,
        out_specs=(vmem, vmem),
        scratch_shapes=[
            pltpu.VMEM((TILES, CHUNK, 2 * LANES), f32),
            pltpu.VMEM((2,) + big, f32),
            pltpu.VMEM((2,) + big, f32),
            pltpu.VMEM((2,) + big, f32),
            pltpu.VMEM((2,) + big, f32),
            pltpu.VMEM((YA // 2, 2 * LANES, 2 * LANES), f32),
            pltpu.VMEM((YA // 2, LANES, 2 * LANES), f32),
            pltpu.VMEM((YA // 2, LANES, 2 * LANES), f32),
            pltpu.VMEM((YA // 2, LANES, 2 * LANES), f32),
            pltpu.VMEM((YA // 2, LANES, 2 * LANES), f32),
            pltpu.VMEM((FREQ, PIECE, NX), f32),
            pltpu.VMEM((2, PIECE, NX), f32),
            pltpu.VMEM((2, ROWS, NX), f32),
            pltpu.VMEM((2, ROWS, NX), f32),
            pltpu.VMEM((2, ROWS, NX), f32),
            pltpu.VMEM((2, ROWS, NX), f32),
            pltpu.VMEM((ROWS, NX), f32),
            pltpu.VMEM((2, FREQ, ROWS, BAND), f32),
            dma((4, CHUNKS)), dma((4, CHUNKS)), dma((4, CHUNKS)),
            dma((1,)), dma((1,)), dma((1,)),
            dma((2,)), dma((2,)),
            dma((2, CHUNKS)), dma((2, CHUNKS)), dma((2, CHUNKS)),
        ],
        compiler_params=pltpu.CompilerParams(
            collective_id=0, has_side_effects=True, vmem_limit_bytes=60 * 2**20
        ),
        name="migrate",
    )(freq_index, owner, wavefield, velocity[0], *tables())
    return image, field


def solution(mesh):
    return jax.shard_map(
        shards,
        mesh=mesh,
        in_specs=(P("freq", None, "space", None), P("freq", "space", None), P("freq"), P()),
        out_specs=(P(None, "space", "freq"), P("freq", None, "space", None)),
        check_vma=False,
    )
```

time: 560 us -> 281 us (0.50)
  Pallas kernels: 0 us -> 272 us
  waiting for transfers between devices: 267 us -> 0 us
  matrix products: 79.7 us -> 0 us
  local copies, waits for them, and re-layouts: 68.1 us -> 4.78 us
  blocking collectives: 59.6 us -> 0 us
  other arithmetic: 37.2 us -> 0 us
  starting transfers between devices: 24.1 us -> 0 us
  between operations: 16.5 us -> 1.28 us
    pallas_call x0 -> x1, Pallas kernels: none -> 272 us  [shards(): pl.pallas_call(kernel, out_shape=(jax.ShapeDtypeStruct((2, ROWS, BAND), f...]
    all_to_all x3 -> x0, waiting for transfers between devices: 173 us -> none  [the longest x2 124 us: shards(): lax.all_to_all(spectrum, 'space', split_axis=2, concat_axis=3, tiled=True)]
    dot_general x16 -> x0, matrix products: 79.7 us -> none  [the longest x2 16 us: shards(): jnp.einsum('fcyab,cbel->feyal', inverse_shaped, inv_xb, precision=highest)]
    all_to_all x1 -> x0, blocking collectives: 59.6 us -> none  [shards(): lax.all_to_all(spectrum, 'space', split_axis=3, concat_axis=2, tiled=True)]
    psum x1 -> x0, waiting for transfers between devices: 55.1 us -> none  [from_root(): return lax.psum(kept, axis)]
    reduce_scatter x2 -> x0, waiting for transfers between devices: 37.6 us -> none  [shards(): lax.psum_scatter(term, 'freq', scatter_dimension=1, tiled=True)]
    transpose x4 -> x0, local copies, waits for them, and re-layouts: 28.5 us -> none  [the longest x2 17.1 us: inverse_y(): return shaped.reshape(count, 2, width_y, 1, narrow)]
    all_to_all x3 -> x0, starting transfers between devices: 24 us -> none  [the longest x2 12 us: shards(): lax.all_to_all(spectrum, 'space', split_axis=2, concat_axis=3, tiled=True)]
  transfers between devices with their start and end apart: 6 -> 0, of which waited for: 5 -> 0; matrix products, arithmetic and copies ran while one was open for 11% -> 0% of each run, Pallas kernels for 0% -> 0%
where the time goes in v1:
time: 281 us; the launch traced here: 278 us
  Pallas kernels  272 us (97%)
  local copies, waits for them, and re-layouts  4.78 us (2%)
    pallas_call x1, Pallas kernels, shards(): pl.pallas_call(kernel, out_shape=(jax.ShapeDtypeStruct((2, ROWS, BAND), f...  272 us

profile of v1, /device:TPU:8, one launch (start us, length us, event | category | flops | bytes accessed | tf_op | source)
XLA Modules:
  0.0 278.3 jit_solution(17090021590129823901)
XLA Ops:
  1.3 272.2 %migrate.1 = (f32[2,64,512]{2,1,0:T(8,128)}, f32[1,2,64,4096]{3,2,1,0:T(8,128)}) custom-call(s32[1]{0:T(128)S(6)} %copy.14.fidx_ref, s32[8]{0:T(128)} %owner_ref.1, f32[1,2,64,4096]{3,2,1,0:T(8,128)} %wave_ref.1, f32[64,4096]{1,0:T(8,128)} %bitcast.1, f32[32,128]{1,0:T(8,128)} %constant.12.clone.txc_ref, f32[32,128]{1,0:T(8,128)} %constant.13.clone.txs_ref, ...), custom_call_target="tpu_custom_call" | custom-call | tf_op jit(solution)/shard_map/migrate/pallas_call | solution.py:414
  273.5 1.7 copy.15
  275.2 3.1 %copy.16 = f32[1,2,64,4096]{3,2,1,0:T(8,128)} copy(f32[1,2,64,4096]{3,2,1,0:T(8,128)} %get-tuple-element.5) | data formatting | bytes 4194304

commit v2 on v1

--- a/solution.py
+++ b/solution.py
@@ -110,56 +110,152 @@
 def kernel(
     fidx_ref, owner_ref, wave_ref, vel_ref, txc_ref, txs_ref, rh_ref, rl_ref, lh_ref, ll_ref,
     image_ref, field_ref,
-    rowbuf, sendx, sendy, recvy, recvx, mid, hcos, hsin, tyc, tys,
-    vrecv, vsel, slow, phc, phs, terms, imag, irecv,
-    asend, arecv, aloc, vsend, vrcv, vloc, gsend, grecv, isend, ircv, iloc,
+    rowbuf, sendx, sendy, recvy, recvx, relay, mid, hcos, hsin, tyc, tys,
+    vrecv, vsel, vpart, vturn, slow, phc, phs, terms, imag, irecv, isum, iback, omega_out, omega_in,
+    asend, arecv, aloc, rsend, rrecv, zsend, zrecv, rloc,
+    vsend, vrcv, vloc, isend, ircv, iloc, tsend, trecv, tloc,
 ):
     f = lax.axis_index("freq")
     me = lax.axis_index("space")
-    zh, yy, cc = me // 8, (me // 2) % 4, me % 2
-
-    def space_peer(j):
-        return ((zh + j // 8) % 4 * 4 + (yy + (j // 2) % 4) % 4) * 2 + (cc + j % 2) % 2
-
-    def freq_peer(j):
-        return (f + j) % FREQ
+    x, zl = f // 2, f % 2
+    zh, y, c = me // 8, (me // 2) % 4, me % 2
+    z = zh * 2 + zl
+    here = (x * 4 + y) * 2 + c
+
+    def dev(dx, dy, dzh, dzl, dc):
+        return (dx * 2 + dzl, (dzh * 4 + dy) * 2 + dc)
+
+    def plane(j):
+        px, py, pc = (x + j // 8) % 4, (y + (j // 2) % 4) % 4, (c + j % 2) % 2
+        return dev(px, py, zh, zl, pc), (px * 4 + py) * 2 + pc
+
+    def along_z(j):
+        pz = (z + j) % 8
+        return dev(x, y, pz // 2, pz % 2, c), pz
+
+    across = dev(zh, y, x, zl, c)
+    across_odd = dev(zh, y, x, 1 - zl, c)
 
     barrier = pltpu.get_barrier_semaphore()
 
-    @pl.loop(1, SPACE)
+    def greet(device):
+        pl.semaphore_signal(barrier, inc=1, device_id=device, device_id_type=MESH)
+
+    @pl.loop(1, 32)
     def _(j):
-        pl.semaphore_signal(barrier, inc=1, device_id=(f, space_peer(j)), device_id_type=MESH)
-
-    @pl.loop(1, FREQ)
+        greet(plane(j)[0])
+
+    @pl.loop(1, 8)
     def _(j):
-        pl.semaphore_signal(barrier, inc=1, device_id=(freq_peer(j), me), device_id_type=MESH)
-
-    pl.semaphore_wait(barrier, SPACE + FREQ - 2)
+        greet(along_z(j)[0])
+
+    @pl.loop(1, 4)
+    def _(j):
+        greet(dev((x + j) % 4, y, zh, 1 - zl, c))
+
+    greet(across_odd)
+
+    @pl.when(x != zh)
+    def _():
+        greet(across)
+
+    @pl.when(x == zh)
+    def _():
+        greet(across_odd)
+
+    pl.semaphore_wait(barrier, 31 + 7 + 3 + 1 + 1)
 
     def remote(src, dst, send, recv, device):
         return pltpu.make_async_remote_copy(
             src_ref=src, dst_ref=dst, send_sem=send, recv_sem=recv, device_id=device, device_id_type=MESH
         )
 
+    def chunk_rows(ch):
+        return pl.ds(ch * CHUNK, CHUNK)
+
     def a2a_start(src, dst, ch, i):
-        rows = pl.ds(ch * CHUNK, CHUNK)
-
-        @pl.loop(1, SPACE)
-        def _(j):
-            d = space_peer(j)
-            remote(src.at[d, rows], dst.at[me, rows], asend.at[i, ch], arecv.at[i, ch], (f, d)).start()
-
-        pltpu.make_async_copy(src.at[me, rows], dst.at[me, rows], aloc.at[i, ch]).start()
-
-    def a2a_all(src, dst, ch, i):
-        rows = pl.ds(ch * CHUNK, CHUNK)
-        some = pl.ds(0, SPACE - 1)
-        return remote(src.at[some, rows], dst.at[some, rows], asend.at[i, ch], arecv.at[i, ch], (f, me))
-
-    def a2a_wait_recv(src, dst, ch, i):
-        rows = pl.ds(ch * CHUNK, CHUNK)
-        a2a_all(src, dst, ch, i).wait_recv()
-        pltpu.make_async_copy(src.at[me, rows], dst.at[me, rows], aloc.at[i, ch]).wait()
+        rows = chunk_rows(ch)
+
+        @pl.loop(1, 32)
+        def _(j):
+            device, place = plane(j)
+            remote(src.at[place, rows], dst.at[here, rows], asend.at[i, ch], arecv.at[i, ch], device).start()
+
+        pltpu.make_async_copy(src.at[here, rows], dst.at[here, rows], aloc.at[i, ch]).start()
+
+    def a2a_all(dst, ch, i):
+        part = dst.at[pl.ds(0, SPACE - 1), chunk_rows(ch)]
+        return remote(part, part, asend.at[i, ch], arecv.at[i, ch], across_odd)
+
+    def a2a_wait_recv(dst, ch, i):
+        a2a_all(dst, ch, i).wait_recv()
+        part = dst.at[here, chunk_rows(ch)]
+        pltpu.make_async_copy(part, part, aloc.at[i, ch]).wait()
+
+    def spread_start(src):
+        @pl.loop(0, 32)
+        def _(j):
+            px, py, pc = (x + (j + zh) % 4) % 4, (y + j // 8) % 4, (c + (j // 4) % 2) % 2
+            place = (px * 4 + py) * 2 + pc
+
+            @pl.when(place != here)
+            def _():
+                remote(src.at[place], relay.at[0, j], rsend.at[0], rrecv.at[0, j], dev(px, py, zh, zl, pc)).start()
+
+    def spread_relay(src, dst):
+        @pl.loop(0, 32)
+        def _(j):
+            px, py, pc = (x + 4 - (j + zh) % 4) % 4, (y + 4 - j // 8) % 4, (c + (j // 4) % 2) % 2
+            place = (px * 4 + py) * 2 + pc
+            slot = (zh * 4 + py) * 2 + pc
+            target = dev(x, y, px, 1 - zl, c)
+
+            @pl.when(place == here)
+            def _():
+                remote(src.at[here], dst.at[slot], zsend.at[0], zrecv.at[0], target).start()
+
+            @pl.when(place != here)
+            def _():
+                remote(relay.at[0, j], relay.at[0, j], rsend.at[0], rrecv.at[0, j], across_odd).wait_recv()
+                remote(relay.at[0, j], dst.at[slot], zsend.at[0], zrecv.at[0], target).start()
+
+    def collect_start(src, ch):
+        rows = chunk_rows(ch)
+
+        @pl.loop(0, 32)
+        def _(j):
+            pzh, py, pc = (zh + j + x) % 4, (y + j // 8) % 4, (c + (j // 4) % 2) % 2
+            remote(
+                src.at[(pzh * 4 + py) * 2 + pc, rows], relay.at[1, j, rows],
+                zsend.at[1 + ch], rrecv.at[1 + ch, j], dev(x, y, pzh, 1 - zl, c),
+            ).start()
+
+    def collect_relay(dst, ch, low, high):
+        rows = chunk_rows(ch)
+
+        @pl.loop(low, high)
+        def _(j):
+            px, py, pc = (zh + 64 - j - x) % 4, (y + j // 8) % 4, (c + (j // 4) % 2) % 2
+            place = (px * 4 + py) * 2 + pc
+            part = relay.at[1, j, rows]
+            remote(part, part, zsend.at[1 + ch], rrecv.at[1 + ch, j], across_odd).wait_recv()
+
+            @pl.when(place == here)
+            def _():
+                pltpu.make_async_copy(part, dst.at[here, rows], rloc.at[ch]).start()
+
+            @pl.when(place != here)
+            def _():
+                remote(part, dst.at[here, rows], rsend.at[1 + ch], zrecv.at[1 + ch], dev(px, py, zh, zl, pc)).start()
+
+    def collect_all(dst, ch):
+        part = dst.at[pl.ds(0, SPACE - 1), chunk_rows(ch)]
+        return remote(part, part, rsend.at[1 + ch], zrecv.at[1 + ch], across_odd)
+
+    def collect_wait_recv(dst, ch):
+        collect_all(dst, ch).wait_recv()
+        part = dst.at[here, chunk_rows(ch)]
+        pltpu.make_async_copy(part, part, rloc.at[ch]).wait()
 
     def forward_x(re_ref, im_ref, dst, ch):
         @pl.loop(0, CHUNK // 8)
@@ -209,7 +305,7 @@
                 re_ref[rows, cols] = re * c - im * s
                 im_ref[rows, cols] = re * s + im * c
 
-    def column_pass(src, dst, i):
+    def column_pass(src, dst, send):
         @pl.loop(0, LANES // 8)
         def _(t):
             half, sub_rows = t // 8, pl.ds(pl.multiple_of(t % 8 * 8, 8), 8)
@@ -253,14 +349,12 @@
                 for a in range(YA):
                     dst[2 * a + half, out_rows, 0:LANES] = vals[a][0]
                     dst[2 * a + half, out_rows, LANES:] = vals[a][1]
-            a2a_start(dst, recvx.at[i // 2], ch, i)
-
-    omega = 2 * math.pi * (lowest_hertz + hertz_step * fidx_ref[0].astype(f32))
-
-    def make_tables():
+            send(ch)
+
+    def make_tables(omega):
         kb = lax.broadcasted_iota(jnp.int32, (LANES, LANES), 0)
         lane = lax.broadcasted_iota(jnp.int32, (LANES, LANES), 1)
-        jx = me + TILES * lane
+        jx = here + TILES * lane
         kx = jnp.where(jx < NX // 2, jx, jx - NX).astype(f32) * (2 * math.pi / (NX * cell_spacing))
 
         @pl.loop(0, YA // 2)
@@ -280,7 +374,7 @@
                 tyc[k, :, cols] = cosine
                 tys[k, :, cols] = sine
 
-    def make_phase(step):
+    def make_phase(step, omega):
         @pl.loop(0, ROWS // 8)
         def _(g):
             rows = pl.ds(pl.multiple_of(g * 8, 8), 8)
@@ -291,106 +385,201 @@
                 phc[step, rows, cols] = cosine
                 phs[step, rows, cols] = sine
 
-    def vel_all(sem):
-        return remote(vrecv.at[pl.ds(0, FREQ - 1)], vrecv.at[pl.ds(0, FREQ - 1)], vsend.at[0], sem, (f, me))
-
-    def gather_all(step):
-        part = slow.at[step, pl.ds(0, (FREQ - 1) * PIECE)]
-        return remote(part, part, gsend.at[step], grecv.at[step], (f, me))
-
-    mine8 = pl.ds(pl.multiple_of(f * PIECE, PIECE), PIECE)
+    quarter = pl.ds(pl.multiple_of(x * 2 * PIECE, 2 * PIECE), 2 * PIECE)
 
     def velocity_start():
-        @pl.loop(1, FREQ)
-        def _(j):
-            p = freq_peer(j)
-            rows = pl.ds(pl.multiple_of(p * PIECE, PIECE), PIECE)
-            remote(vel_ref.at[rows], vrecv.at[f], vsend.at[0], vrcv.at[0], (p, me)).start()
-        pltpu.make_async_copy(vel_ref.at[mine8], vrecv.at[f], vloc.at[0]).start()
-
-    def velocity_share():
-        vel_all(vrcv.at[0]).wait_recv()
-        pltpu.make_async_copy(vel_ref.at[mine8], vrecv.at[f], vloc.at[0]).wait()
+        @pl.loop(1, 4)
+        def _(j):
+            px = (x + j) % 4
+            rows = pl.ds(pl.multiple_of(px * 2 * PIECE, 2 * PIECE), 2 * PIECE)
+            remote(vel_ref.at[rows], vrecv.at[x], vsend.at[0], vrcv.at[0], dev(px, y, zh, zl, c)).start()
+
+        pltpu.make_async_copy(vel_ref.at[quarter], vrecv.at[x], vloc.at[0]).start()
+
+    def velocity_all():
+        part = vrecv.at[pl.ds(0, 3)]
+        return remote(part, part, vsend.at[0], vrcv.at[0], across_odd)
+
+    partner = dev(x, y, zh, 1 - zl, c)
+    own_half = pl.ds(pl.multiple_of(zl * PIECE, PIECE), PIECE)
+    other_half = pl.ds(pl.multiple_of((1 - zl) * PIECE, PIECE), PIECE)
+    pair0 = remote(vsel.at[0, other_half], vpart.at[0, pl.ds(0, PIECE)], vsend.at[1], vrcv.at[1], partner)
+    pair1 = remote(vsel.at[1], vpart.at[1], vsend.at[2], vrcv.at[2], partner)
+    turn = remote(vsel.at[2, pl.ds(0, PIECE)], vturn, vsend.at[3], vrcv.at[3], across)
+    turn_here = pltpu.make_async_copy(vsel.at[2, pl.ds(0, PIECE)], vturn, vloc.at[1])
+
+    def velocity_select():
+        velocity_all().wait_recv()
+        pltpu.make_async_copy(vel_ref.at[quarter], vrecv.at[x], vloc.at[0]).wait()
         for step in range(2):
-            piece = 1.0 / vrecv[owner_ref[step]] - 1.0 / base_speed
-            vsel[step] = piece
-            slow[step, mine8] = piece
-
-            @pl.loop(1, FREQ)
-            def _(j):
-                remote(vsel.at[step], slow.at[step, mine8], gsend.at[step], grecv.at[step], (freq_peer(j), me)).start()
+            chosen = owner_ref[step]
+            piece = 1.0 / vrecv[chosen // 2] - 1.0 / base_speed
+            vsel[step] = jnp.where(chosen % 2 == zl, piece, 0.0)
+        pair0.start()
+        pair0.wait_recv()
+        vsel[2, 0:PIECE] = vsel[0, own_half] + vpart[0, 0:PIECE]
+
+        @pl.when(x != zh)
+        def _():
+            turn.start()
+            turn.wait_recv()
+
+        @pl.when(x == zh)
+        def _():
+            turn_here.start()
+            turn_here.wait()
+
+    eighth = pl.ds(pl.multiple_of(z * PIECE, PIECE), PIECE)
+
+    def velocity_along_z():
+        @pl.loop(1, 8)
+        def _(j):
+            remote(vturn, slow.at[0, eighth], vsend.at[4], vrcv.at[4], along_z(j)[0]).start()
+
+        slow[0, eighth] = vturn[...]
+        pair1.start()
+
+    def along_z_all():
+        part = slow.at[0, pl.ds(0, 7 * PIECE)]
+        return remote(part, part, vsend.at[4], vrcv.at[4], across_odd)
+
+    def velocity_along_x():
+        pair1.wait_recv()
+        piece = vsel[1] + vpart[1]
+        vsel[3] = piece
+        slow[1, quarter] = piece
+
+        @pl.loop(1, 4)
+        def _(j):
+            remote(vsel.at[3], slow.at[1, quarter], vsend.at[5], vrcv.at[5], dev((x + j) % 4, y, zh, zl, c)).start()
+
+    def along_x_all():
+        part = slow.at[1, pl.ds(0, 6 * PIECE)]
+        return remote(part, part, vsend.at[5], vrcv.at[5], across_odd)
 
     def image_start(step, ch):
-        rows = pl.ds(ch * CHUNK, CHUNK)
-
-        @pl.loop(1, FREQ)
-        def _(j):
-            p = freq_peer(j)
+        rows = chunk_rows(ch)
+        mine = z if step == 0 else f
+
+        @pl.loop(1, 8)
+        def _(j):
+            if step == 0:
+                device, p = along_z(j)
+            else:
+                p = (f + j) % 8
+                device = (p, me)
             cols = pl.ds(pl.multiple_of(p * BAND, BAND), BAND)
             remote(
-                terms.at[step, rows, cols], irecv.at[step, f, rows],
-                isend.at[step, ch], ircv.at[step, ch], (p, me),
+                terms.at[step, rows, cols], irecv.at[step, mine, rows],
+                isend.at[step, ch], ircv.at[step, ch], device,
             ).start()
 
-        cols = pl.ds(pl.multiple_of(f * BAND, BAND), BAND)
-        pltpu.make_async_copy(terms.at[step, rows, cols], irecv.at[step, f, rows], iloc.at[step, ch]).start()
+        cols = pl.ds(pl.multiple_of(mine * BAND, BAND), BAND)
+        pltpu.make_async_copy(terms.at[step, rows, cols], irecv.at[step, mine, rows], iloc.at[step, ch]).start()
 
     def image_all(step, ch):
-        part = irecv.at[step, pl.ds(0, FREQ - 1), pl.ds(ch * CHUNK, CHUNK)]
-        return remote(part, part, isend.at[step, ch], ircv.at[step, ch], (f, me))
-
-    def image_finish(step, ch):
-        rows = pl.ds(ch * CHUNK, CHUNK)
+        part = irecv.at[step, pl.ds(0, FREQ - 1), chunk_rows(ch)]
+        return remote(part, part, isend.at[step, ch], ircv.at[step, ch], across_odd)
+
+    def image_sum(step, ch):
+        rows = chunk_rows(ch)
         image_all(step, ch).wait_recv()
         part = irecv.at[step, 0, rows]
         pltpu.make_async_copy(part, part, iloc.at[step, ch]).wait()
         total = irecv[step, 0, rows, :]
         for j in range(1, FREQ):
             total = total + irecv[step, j, rows, :]
-        image_ref[step, rows, :] = total
-
-    velocity_start()
+        return rows, total
+
+    back = remote(isum, iback, tsend.at[0], trecv.at[0], across)
+    back_here = pltpu.make_async_copy(isum, iback, tloc.at[0])
+
+    omega = 2 * math.pi * (lowest_hertz + hertz_step * fidx_ref[0].astype(f32))
+    omega_out[...] = jnp.full((8, LANES), omega, f32)
+    omega_turn = remote(omega_out, omega_in, tsend.at[1], trecv.at[1], across_odd)
+    omega_turn.start()
     for ch in range(CHUNKS):
         forward_x(wave_ref.at[0, 0], wave_ref.at[0, 1], sendx.at[0], ch)
-        a2a_start(sendx.at[0], recvy.at[0], ch, 0)
-    make_tables()
-    velocity_share()
-    gather_all(0).wait_recv()
-    gather_all(1).wait_recv()
-    make_phase(0)
-    make_phase(1)
+    spread_start(sendx.at[0])
+    velocity_start()
+    spread_relay(sendx.at[0], recvy.at[0])
+    omega_turn.wait_recv()
+    omega_col = omega_in[0:1, :]
+    make_tables(omega_col)
+    velocity_select()
+    recvy_all = remote(recvy.at[0], recvy.at[0], zsend.at[0], zrecv.at[0], across_odd)
+    recvy_all.wait_recv()
+    velocity_along_z()
+    column_pass(recvy.at[0], sendy.at[0], lambda ch: a2a_start(sendy.at[0], recvx.at[0], ch, 0))
+    along_z_all().wait_recv()
+    make_phase(0, omega_in[0:1, 0:1])
     for ch in range(CHUNKS):
-        a2a_wait_recv(sendx.at[0], recvy.at[0], ch, 0)
-    column_pass(recvy.at[0], sendy.at[0], 1)
-    for ch in range(CHUNKS):
-        a2a_wait_recv(sendy.at[0], recvx.at[0], ch, 1)
+        a2a_wait_recv(recvx.at[0], ch, 0)
         inverse_x(recvx.at[0], 0, terms.at[0], imag, ch)
         forward_x(terms.at[0], imag, sendx.at[1], ch)
-        a2a_start(sendx.at[1], recvy.at[1], ch, 2)
+        a2a_start(sendx.at[1], recvy.at[1], ch, 1)
         image_start(0, ch)
     for ch in range(CHUNKS):
-        a2a_wait_recv(sendx.at[1], recvy.at[1], ch, 2)
-    column_pass(recvy.at[1], sendy.at[1], 3)
+        a2a_wait_recv(recvy.at[1], ch, 1)
+    column_pass(recvy.at[1], sendy.at[1], lambda ch: collect_start(sendy.at[1], ch))
+    velocity_along_x()
     for ch in range(CHUNKS):
-        image_finish(0, ch)
-    for ch in range(CHUNKS):
-        a2a_wait_recv(sendy.at[1], recvx.at[1], ch, 3)
+        rows, total = image_sum(0, ch)
+        isum[rows, :] = total
+
+    @pl.when(x != zh)
+    def _():
+        back.start()
+
+    @pl.when(x == zh)
+    def _():
+        back_here.start()
+
+    def finish(ch):
+        collect_wait_recv(recvx.at[1], ch)
         inverse_x(recvx.at[1], 1, terms.at[1], field_ref.at[0, 1], ch)
         image_start(1, ch)
-        rows = slice(ch * CHUNK, (ch + 1) * CHUNK)
+        rows = chunk_rows(ch)
         field_ref[0, 0, rows, :] = terms[1, rows, :]
+
+    collect_relay(recvx.at[1], 0, 0, 32)
+    along_x_all().wait_recv()
+    make_phase(1, omega)
+    for ch in range(1, CHUNKS):
+        collect_relay(recvx.at[1], ch, 0, 16)
+        finish(ch - 1)
+        collect_relay(recvx.at[1], ch, 16, 32)
+    finish(CHUNKS - 1)
+
+    @pl.when(x != zh)
+    def _():
+        back.wait()
+        turn.wait_send()
+
+    @pl.when(x == zh)
+    def _():
+        back_here.wait()
+
+    image_ref[0] = iback[...]
     for ch in range(CHUNKS):
-        image_finish(1, ch)
-
-    vel_all(vrcv.at[0]).wait_send()
-    for step in range(2):
-        remote(slow.at[step, pl.ds(0, (FREQ - 1) * PIECE)], slow.at[step, pl.ds(0, (FREQ - 1) * PIECE)], gsend.at[step], grecv.at[step], (f, me)).wait_send()
+        rows, total = image_sum(1, ch)
+        image_ref[1, rows, :] = total
+
+    omega_turn.wait_send()
+    remote(relay.at[0, pl.ds(0, 31)], relay.at[0, pl.ds(0, 31)], rsend.at[0], rrecv.at[0, 0], across_odd).wait_send()
+    recvy_all.wait_send()
+    velocity_all().wait_send()
+    pair0.wait_send()
+    pair1.wait_send()
+    along_z_all().wait_send()
+    along_x_all().wait_send()
     for ch in range(CHUNKS):
-        for i in range(4):
-            src = (sendx if i % 2 == 0 else sendy).at[i // 2]
-            a2a_all(src, src, ch, i).wait_send()
-        for step in range(2):
-            image_all(step, ch).wait_send()
+        part = relay.at[1, :, chunk_rows(ch)]
+        remote(part, part, zsend.at[1 + ch], rrecv.at[1 + ch, 0], across_odd).wait_send()
+        collect_all(recvx.at[1], ch).wait_send()
+        for i in range(2):
+            a2a_all(recvx.at[0], ch, i).wait_send()
+            image_all(i, ch).wait_send()
 
 
 def tables():
@@ -425,23 +614,31 @@
             pltpu.VMEM((2,) + big, f32),
             pltpu.VMEM((2,) + big, f32),
             pltpu.VMEM((2,) + big, f32),
+            pltpu.VMEM((2,) + big, f32),
             pltpu.VMEM((YA // 2, 2 * LANES, 2 * LANES), f32),
             pltpu.VMEM((YA // 2, LANES, 2 * LANES), f32),
             pltpu.VMEM((YA // 2, LANES, 2 * LANES), f32),
             pltpu.VMEM((YA // 2, LANES, 2 * LANES), f32),
             pltpu.VMEM((YA // 2, LANES, 2 * LANES), f32),
-            pltpu.VMEM((FREQ, PIECE, NX), f32),
-            pltpu.VMEM((2, PIECE, NX), f32),
+            pltpu.VMEM((4, 2 * PIECE, NX), f32),
+            pltpu.VMEM((4, 2 * PIECE, NX), f32),
+            pltpu.VMEM((2, 2 * PIECE, NX), f32),
+            pltpu.VMEM((PIECE, NX), f32),
             pltpu.VMEM((2, ROWS, NX), f32),
             pltpu.VMEM((2, ROWS, NX), f32),
             pltpu.VMEM((2, ROWS, NX), f32),
             pltpu.VMEM((2, ROWS, NX), f32),
             pltpu.VMEM((ROWS, NX), f32),
             pltpu.VMEM((2, FREQ, ROWS, BAND), f32),
-            dma((4, CHUNKS)), dma((4, CHUNKS)), dma((4, CHUNKS)),
-            dma((1,)), dma((1,)), dma((1,)),
-            dma((2,)), dma((2,)),
+            pltpu.VMEM((ROWS, BAND), f32),
+            pltpu.VMEM((ROWS, BAND), f32),
+            pltpu.VMEM((8, LANES), f32),
+            pltpu.VMEM((8, LANES), f32),
             dma((2, CHUNKS)), dma((2, CHUNKS)), dma((2, CHUNKS)),
+            dma((1 + CHUNKS,)), dma((1 + CHUNKS, 32)), dma((1 + CHUNKS,)), dma((1 + CHUNKS,)), dma((CHUNKS,)),
+            dma((6,)), dma((6,)), dma((2,)),
+            dma((2, CHUNKS)), dma((2, CHUNKS)), dma((2, CHUNKS)),
+            dma((2,)), dma((2,)), dma((1,)),
         ],
         compiler_params=pltpu.CompilerParams(
             collective_id=0, has_side_effects=True, vmem_limit_bytes=60 * 2**20

time: 281 us -> 230 us (0.82)
  the two profiles are of different devices: /device:TPU:8 before, /device:TPU:27 now
where the time goes in v2:
time: 230 us
  Pallas kernels  224 us (97%)
  local copies, waits for them, and re-layouts  4.78 us (2%)
    pallas_call x1, Pallas kernels, shards(): pl.pallas_call(kernel, out_shape=(jax.ShapeDtypeStruct((2, ROWS, BAND), f...  224 us
    unnamed x2, local copies, waits for them, and re-layouts  4.78 us

profile of v2, /device:TPU:27, one launch (start us, length us, event | category | flops | bytes accessed | tf_op | source)
XLA Modules:
  0.0 230.3 jit_solution(9190784631618557013)
XLA Ops:
  1.3 224.2 %migrate.1 = (f32[2,64,512]{2,1,0:T(8,128)}, f32[1,2,64,4096]{3,2,1,0:T(8,128)}) custom-call(s32[1]{0:T(128)S(6)} %copy.14.fidx_ref, s32[8]{0:T(128)} %owner_ref.1, f32[1,2,64,4096]{3,2,1,0:T(8,128)} %wave_ref.1, f32[64,4096]{1,0:T(8,128)} %bitcast.1, f32[32,128]{1,0:T(8,128)} %constant.12.clone.txc_ref, f32[32,128]{1,0:T(8,128)} %constant.13.clone.txs_ref, ...), custom_call_target="tpu_custom_call" | custom-call | tf_op jit(solution)/shard_map/migrate/pallas_call | solution.py:603
  225.5 1.7 copy.15
  227.2 3.1 %copy.16 = f32[1,2,64,4096]{3,2,1,0:T(8,128)} copy(f32[1,2,64,4096]{3,2,1,0:T(8,128)} %get-tuple-element.5) | data formatting | bytes 4194304

commit v3 on v2

--- a/solution.py
+++ b/solution.py
@@ -20,6 +20,7 @@
 CHUNKS = ROWS // CHUNK
 BAND = NX // FREQ
 PIECE = ROWS // FREQ
+AHEAD, BEHIND, WINDOW = 16, 16, 16
 
 cell_spacing = 25.0
 layer_thickness = 10.0
@@ -107,13 +108,21 @@
     return dot(ah, bh) + (dot(al, bh) + dot(ah, bl))
 
 
+def left_mul3(left_ref, b):
+    bh, bl = b
+    n = bh.shape[0]
+    dot = functools.partial(jnp.dot, preferred_element_type=f32)
+    both = dot(left_ref[...], bh)
+    return both[:n] + (both[n:] + dot(left_ref[:n, :], bl))
+
+
 def kernel(
-    fidx_ref, owner_ref, wave_ref, vel_ref, txc_ref, txs_ref, rh_ref, rl_ref, lh_ref, ll_ref,
+    fidx_ref, owner_ref, wave_ref, vel_ref, txc_ref, txs_ref, rh_ref, rl_ref, lh_ref, ll_ref, rs_ref, ls_ref,
     image_ref, field_ref,
     rowbuf, sendx, sendy, recvy, recvx, relay, mid, hcos, hsin, tyc, tys,
     vrecv, vsel, vpart, vturn, slow, phc, phs, terms, imag, irecv, isum, iback, omega_out, omega_in,
     asend, arecv, aloc, rsend, rrecv, zsend, zrecv, rloc,
-    vsend, vrcv, vloc, isend, ircv, iloc, tsend, trecv, tloc,
+    vsend, vrcv, vloc, isend, ircv, iloc, tsend, trecv, tloc, gate, csend, psend,
 ):
     f = lax.axis_index("freq")
     me = lax.axis_index("space")
@@ -126,13 +135,14 @@
         return (dx * 2 + dzl, (dzh * 4 + dy) * 2 + dc)
 
     def plane(j):
-        px, py, pc = (x + j // 8) % 4, (y + (j // 2) % 4) % 4, (c + j % 2) % 2
+        px, py, pc = (x + j % 4) % 4, (y + j // 4 + j) % 4, (c + j // 16) % 2
         return dev(px, py, zh, zl, pc), (px * 4 + py) * 2 + pc
 
     def along_z(j):
         pz = (z + j) % 8
         return dev(x, y, pz // 2, pz % 2, c), pz
 
+    other_core = dev(x, y, zh, zl, 1 - c)
     across = dev(zh, y, x, zl, c)
     across_odd = dev(zh, y, x, 1 - zl, c)
 
@@ -162,8 +172,6 @@
     @pl.when(x == zh)
     def _():
         greet(across_odd)
-
-    pl.semaphore_wait(barrier, 31 + 7 + 3 + 1 + 1)
 
     def remote(src, dst, send, recv, device):
         return pltpu.make_async_remote_copy(
@@ -183,6 +191,36 @@
 
         pltpu.make_async_copy(src.at[here, rows], dst.at[here, rows], aloc.at[i, ch]).start()
 
+    def a2a_start_core(src, dst, ch, i, core):
+        rows = chunk_rows(ch)
+
+        @pl.loop(0, 16)
+        def _(k):
+            px, py = (x + k % 4) % 4, (y + k // 4 + k) % 4
+            place = (px * 4 + py) * 2 + core
+
+            @pl.when(place != here)
+            def _():
+                remote(
+                    src.at[place, rows], dst.at[here, rows], csend.at[core, ch], arecv.at[i, ch],
+                    dev(px, py, zh, zl, core),
+                ).start()
+
+            @pl.when(place == here)
+            def _():
+                pltpu.make_async_copy(src.at[here, rows], dst.at[here, rows], aloc.at[i, ch]).start()
+
+    def a2a_core_sent(dst, ch, i, core):
+        @pl.when(c == core)
+        def _():
+            part = dst.at[pl.ds(0, 15), chunk_rows(ch)]
+            remote(part, part, csend.at[core, ch], arecv.at[i, ch], across_odd).wait_send()
+
+        @pl.when(c != core)
+        def _():
+            part = dst.at[pl.ds(0, 16), chunk_rows(ch)]
+            remote(part, part, csend.at[core, ch], arecv.at[i, ch], across_odd).wait_send()
+
     def a2a_all(dst, ch, i):
         part = dst.at[pl.ds(0, SPACE - 1), chunk_rows(ch)]
         return remote(part, part, asend.at[i, ch], arecv.at[i, ch], across_odd)
@@ -192,61 +230,110 @@
         part = dst.at[here, chunk_rows(ch)]
         pltpu.make_async_copy(part, part, aloc.at[i, ch]).wait()
 
-    def spread_start(src):
+    def spread_send(src, q, sent=False):
+        k, pc = q % 16, q // 16
+        px, py = (x + k + zh) % 4, (y + k // 4 + k) % 4
+        place, slot = (px * 4 + py) * 2 + pc, k * 2 + c
+
+        @pl.when(place != here)
+        def _():
+            copy = remote(
+                src.at[place], relay.at[0, slot], psend.at[q], rrecv.at[0, slot], dev(px, py, zh, zl, pc)
+            )
+            if sent:
+                copy.wait_send()
+            else:
+                copy.start()
+
+    def spread_relay(src, dst, r):
+        k, pc = r // 2, r % 2
+        px, py = (x + 64 - k - zh) % 4, (y + 64 - k // 4 - k) % 4
+        place, slot = (px * 4 + py) * 2 + pc, (zh * 4 + py) * 2 + pc
+        target = dev(x, y, px, 1 - zl, c)
+
+        @pl.when(place == here)
+        def _():
+            remote(src.at[here], dst.at[slot], zsend.at[0], zrecv.at[0], target).start()
+
+        @pl.when(place != here)
+        def _():
+            remote(relay.at[0, r], relay.at[0, r], rsend.at[0], rrecv.at[0, r], across_odd).wait_recv()
+            remote(relay.at[0, r], dst.at[slot], zsend.at[0], zrecv.at[0], target).start()
+
+    def spread(src, dst):
+        ahead = AHEAD + (32 - AHEAD) * c
+
+        @pl.loop(0, ahead)
+        def _(q):
+            @pl.when(q >= WINDOW)
+            def _():
+                spread_send(src, q - WINDOW, True)
+
+            spread_send(src, q)
+
+        @pl.when(c == 1)
+        def _():
+            @pl.loop(32 - WINDOW, 32)
+            def _(q):
+                spread_send(src, q, True)
+
+            velocity_start()
+            pl.semaphore_wait(gate.at[0], 1)
+
         @pl.loop(0, 32)
-        def _(j):
-            px, py, pc = (x + (j + zh) % 4) % 4, (y + j // 8) % 4, (c + (j // 4) % 2) % 2
-            place = (px * 4 + py) * 2 + pc
-
-            @pl.when(place != here)
+        def _(r):
+            spread_relay(src, dst, r)
+
+            @pl.when((c == 0) & (r == 12))
             def _():
-                remote(src.at[place], relay.at[0, j], rsend.at[0], rrecv.at[0, j], dev(px, py, zh, zl, pc)).start()
-
-    def spread_relay(src, dst):
-        @pl.loop(0, 32)
-        def _(j):
-            px, py, pc = (x + 4 - (j + zh) % 4) % 4, (y + 4 - j // 8) % 4, (c + (j // 4) % 2) % 2
-            place = (px * 4 + py) * 2 + pc
-            slot = (zh * 4 + py) * 2 + pc
-            target = dev(x, y, px, 1 - zl, c)
-
-            @pl.when(place == here)
+                velocity_start()
+
+            @pl.when(ahead + r < 32)
             def _():
-                remote(src.at[here], dst.at[slot], zsend.at[0], zrecv.at[0], target).start()
-
-            @pl.when(place != here)
+                spread_send(src, ahead + r - WINDOW, True)
+                spread_send(src, ahead + r)
+
+        @pl.when(c == 0)
+        def _():
+            @pl.loop(32 - WINDOW, 32)
+            def _(q):
+                spread_send(src, q, True)
+
+            pl.semaphore_signal(gate.at[0], inc=1, device_id=other_core, device_id_type=MESH)
+
+    def collect_send(src, i):
+        ch, j = i // 32, i % 32
+        rows = pl.ds(pl.multiple_of(ch * CHUNK, CHUNK), CHUNK)
+        pzh, py, pc = (zh + j + x) % 4, (y + j // 8) % 4, (c + (j // 4) % 2) % 2
+        remote(
+            src.at[(pzh * 4 + py) * 2 + pc, rows], relay.at[1, j, rows],
+            zsend.at[1 + ch], rrecv.at[1 + ch, j], dev(x, y, pzh, 1 - zl, c),
+        ).start()
+
+    def collect_relay(dst, i):
+        ch, j = i // 32, i % 32
+        rows = pl.ds(pl.multiple_of(ch * CHUNK, CHUNK), CHUNK)
+        px, py, pc = (zh + 64 - j - x) % 4, (y + j // 8) % 4, (c + (j // 4) % 2) % 2
+        place = (px * 4 + py) * 2 + pc
+        part = relay.at[1, j, rows]
+        remote(part, part, zsend.at[1 + ch], rrecv.at[1 + ch, j], across_odd).wait_recv()
+
+        @pl.when(place == here)
+        def _():
+            pltpu.make_async_copy(part, dst.at[here, rows], rloc.at[ch]).start()
+
+        @pl.when(place != here)
+        def _():
+            remote(part, dst.at[here, rows], rsend.at[1 + ch], zrecv.at[1 + ch], dev(px, py, zh, zl, pc)).start()
+
+    def collect(src, dst, low, high):
+        @pl.loop(low, high)
+        def _(i):
+            collect_relay(dst, i)
+
+            @pl.when(BEHIND + i < 32 * CHUNKS)
             def _():
-                remote(relay.at[0, j], relay.at[0, j], rsend.at[0], rrecv.at[0, j], across_odd).wait_recv()
-                remote(relay.at[0, j], dst.at[slot], zsend.at[0], zrecv.at[0], target).start()
-
-    def collect_start(src, ch):
-        rows = chunk_rows(ch)
-
-        @pl.loop(0, 32)
-        def _(j):
-            pzh, py, pc = (zh + j + x) % 4, (y + j // 8) % 4, (c + (j // 4) % 2) % 2
-            remote(
-                src.at[(pzh * 4 + py) * 2 + pc, rows], relay.at[1, j, rows],
-                zsend.at[1 + ch], rrecv.at[1 + ch, j], dev(x, y, pzh, 1 - zl, c),
-            ).start()
-
-    def collect_relay(dst, ch, low, high):
-        rows = chunk_rows(ch)
-
-        @pl.loop(low, high)
-        def _(j):
-            px, py, pc = (zh + 64 - j - x) % 4, (y + j // 8) % 4, (c + (j // 4) % 2) % 2
-            place = (px * 4 + py) * 2 + pc
-            part = relay.at[1, j, rows]
-            remote(part, part, zsend.at[1 + ch], rrecv.at[1 + ch, j], across_odd).wait_recv()
-
-            @pl.when(place == here)
-            def _():
-                pltpu.make_async_copy(part, dst.at[here, rows], rloc.at[ch]).start()
-
-            @pl.when(place != here)
-            def _():
-                remote(part, dst.at[here, rows], rsend.at[1 + ch], zrecv.at[1 + ch], dev(px, py, zh, zl, pc)).start()
+                collect_send(src, BEHIND + i)
 
     def collect_all(dst, ch):
         part = dst.at[pl.ds(0, SPACE - 1), chunk_rows(ch)]
@@ -324,12 +411,11 @@
 
         @pl.loop(0, YA // 2)
         def _(k):
-            left = (lh_ref[...], ll_ref[...])
-            spec = mul3(left, split(mid[k]))
+            spec = left_mul3(ls_ref, split(mid[k]))
             re, im = spec[:LANES], spec[LANES:]
             c, s = hcos[k], hsin[k]
             spec = jnp.concatenate([re * c - im * s, re * s + im * c], axis=0)
-            mid[k] = mul3((rh_ref[...], rl_ref[...]), split(spec))
+            mid[k] = left_mul3(rs_ref, split(spec))
 
         for ch in range(CHUNKS):
             @pl.loop(0, CHUNK // 4)
@@ -351,6 +437,17 @@
                     dst[2 * a + half, out_rows, LANES:] = vals[a][1]
             send(ch)
 
+    def make_twiddles():
+        kb = lax.broadcasted_iota(jnp.int32, (LANES, LANES), 0)
+
+        @pl.loop(0, YA // 2)
+        def _(k):
+            for part in range(2):
+                cols = slice(part * LANES, (part + 1) * LANES)
+                sine, cosine = sin_cos(((2 * k + part) * kb).astype(f32) * (2 * math.pi / NY))
+                tyc[k, :, cols] = cosine
+                tys[k, :, cols] = sine
+
     def make_tables(omega):
         kb = lax.broadcasted_iota(jnp.int32, (LANES, LANES), 0)
         lane = lax.broadcasted_iota(jnp.int32, (LANES, LANES), 1)
@@ -370,9 +467,6 @@
                 sine, cosine = sin_cos(jnp.where(vertical > 0.0, root, 0.0))
                 hcos[k, :, cols] = damping * cosine
                 hsin[k, :, cols] = damping * sine
-                sine, cosine = sin_cos((ka * kb).astype(f32) * (2 * math.pi / NY))
-                tyc[k, :, cols] = cosine
-                tys[k, :, cols] = sine
 
     def make_phase(step, omega):
         @pl.loop(0, ROWS // 8)
@@ -416,18 +510,29 @@
             piece = 1.0 / vrecv[chosen // 2] - 1.0 / base_speed
             vsel[step] = jnp.where(chosen % 2 == zl, piece, 0.0)
         pair0.start()
+
+    def velocity_turn():
         pair0.wait_recv()
         vsel[2, 0:PIECE] = vsel[0, own_half] + vpart[0, 0:PIECE]
 
         @pl.when(x != zh)
         def _():
             turn.start()
+
+        @pl.when(x == zh)
+        def _():
+            turn_here.start()
+
+    def velocity_spread():
+        @pl.when(x != zh)
+        def _():
             turn.wait_recv()
 
         @pl.when(x == zh)
         def _():
-            turn_here.start()
             turn_here.wait()
+
+        velocity_along_z()
 
     eighth = pl.ds(pl.multiple_of(z * PIECE, PIECE), PIECE)
 
@@ -437,7 +542,6 @@
             remote(vturn, slow.at[0, eighth], vsend.at[4], vrcv.at[4], along_z(j)[0]).start()
 
         slow[0, eighth] = vturn[...]
-        pair1.start()
 
     def along_z_all():
         part = slow.at[0, pl.ds(0, 7 * PIECE)]
@@ -497,31 +601,61 @@
     omega = 2 * math.pi * (lowest_hertz + hertz_step * fidx_ref[0].astype(f32))
     omega_out[...] = jnp.full((8, LANES), omega, f32)
     omega_turn = remote(omega_out, omega_in, tsend.at[1], trecv.at[1], across_odd)
-    omega_turn.start()
     for ch in range(CHUNKS):
         forward_x(wave_ref.at[0, 0], wave_ref.at[0, 1], sendx.at[0], ch)
-    spread_start(sendx.at[0])
-    velocity_start()
-    spread_relay(sendx.at[0], recvy.at[0])
+    make_twiddles()
+    pl.semaphore_wait(barrier, 31 + 7 + 3 + 1 + 1)
+    omega_turn.start()
+    spread(sendx.at[0], recvy.at[0])
     omega_turn.wait_recv()
     omega_col = omega_in[0:1, :]
+    velocity_select()
     make_tables(omega_col)
-    velocity_select()
     recvy_all = remote(recvy.at[0], recvy.at[0], zsend.at[0], zrecv.at[0], across_odd)
+
+    @pl.when(c == 1)
+    def _():
+        velocity_turn()
+
     recvy_all.wait_recv()
-    velocity_along_z()
+    pl.semaphore_signal(gate.at[1], inc=1, device_id=other_core, device_id_type=MESH)
+
+    @pl.when(c == 1)
+    def _():
+        pl.semaphore_wait(gate.at[1], 1)
+        velocity_spread()
+
     column_pass(recvy.at[0], sendy.at[0], lambda ch: a2a_start(sendy.at[0], recvx.at[0], ch, 0))
+
+
+    @pl.when(c == 0)
+    def _():
+        velocity_turn()
+        pl.semaphore_wait(gate.at[1], 1)
+        velocity_spread()
+
     along_z_all().wait_recv()
     make_phase(0, omega_in[0:1, 0:1])
     for ch in range(CHUNKS):
         a2a_wait_recv(recvx.at[0], ch, 0)
         inverse_x(recvx.at[0], 0, terms.at[0], imag, ch)
         forward_x(terms.at[0], imag, sendx.at[1], ch)
-        a2a_start(sendx.at[1], recvy.at[1], ch, 1)
+        a2a_start_core(sendx.at[1], recvy.at[1], ch, 1, 0)
         image_start(0, ch)
     for ch in range(CHUNKS):
+        a2a_core_sent(sendx.at[1], ch, 1, 0)
+        a2a_start_core(sendx.at[1], recvy.at[1], ch, 1, 1)
+    pair1.start()
+    for ch in range(CHUNKS):
         a2a_wait_recv(recvy.at[1], ch, 1)
-    column_pass(recvy.at[1], sendy.at[1], lambda ch: collect_start(sendy.at[1], ch))
+
+    def collect_first(ch):
+        if ch == 0:
+            @pl.loop(0, BEHIND)
+            def _(i):
+                collect_send(sendy.at[1], i)
+
+    column_pass(recvy.at[1], sendy.at[1], collect_first)
     velocity_along_x()
     for ch in range(CHUNKS):
         rows, total = image_sum(0, ch)
@@ -542,13 +676,13 @@
         rows = chunk_rows(ch)
         field_ref[0, 0, rows, :] = terms[1, rows, :]
 
-    collect_relay(recvx.at[1], 0, 0, 32)
+    collect(sendy.at[1], recvx.at[1], 0, 32)
     along_x_all().wait_recv()
     make_phase(1, omega)
     for ch in range(1, CHUNKS):
-        collect_relay(recvx.at[1], ch, 0, 16)
+        collect(sendy.at[1], recvx.at[1], 32 * ch, 32 * ch + 16)
         finish(ch - 1)
-        collect_relay(recvx.at[1], ch, 16, 32)
+        collect(sendy.at[1], recvx.at[1], 32 * ch + 16, 32 * ch + 32)
     finish(CHUNKS - 1)
 
     @pl.when(x != zh)
@@ -566,7 +700,6 @@
         image_ref[1, rows, :] = total
 
     omega_turn.wait_send()
-    remote(relay.at[0, pl.ds(0, 31)], relay.at[0, pl.ds(0, 31)], rsend.at[0], rrecv.at[0, 0], across_odd).wait_send()
     recvy_all.wait_send()
     velocity_all().wait_send()
     pair0.wait_send()
@@ -577,9 +710,10 @@
         part = relay.at[1, :, chunk_rows(ch)]
         remote(part, part, zsend.at[1 + ch], rrecv.at[1 + ch, 0], across_odd).wait_send()
         collect_all(recvx.at[1], ch).wait_send()
-        for i in range(2):
-            a2a_all(recvx.at[0], ch, i).wait_send()
-            image_all(i, ch).wait_send()
+        a2a_all(recvx.at[0], ch, 0).wait_send()
+        a2a_core_sent(sendx.at[1], ch, 1, 1)
+        for step in range(2):
+            image_all(step, ch).wait_send()
 
 
 def tables():
@@ -591,8 +725,32 @@
     for m in (right, right.T):
         high = m.astype(ml_dtypes.bfloat16)
         out += [high, (m - high.astype(np.float64)).astype(ml_dtypes.bfloat16)]
+    out += [np.concatenate(out[:2]), np.concatenate(out[2:4])]
     tx = 2 * np.pi * ((np.arange(TILES)[:, None] * n[None, :]) % NX) / NX
     return [np.cos(tx).astype(np.float32), np.sin(tx).astype(np.float32)] + out
+
+
+def hand_kernel(image_in, field_in, image_out, field_out):
+    image_out[...] = image_in[...]
+    field_out[...] = field_in[...]
+
+
+def hand_over(image, field):
+    specs = (
+        pl.BlockSpec((2, ROWS // 4, BAND), lambda i: (0, i, 0)),
+        pl.BlockSpec((1, 2, ROWS // 4, NX), lambda i: (0, 0, i, 0)),
+    )
+    return pl.pallas_call(
+        hand_kernel,
+        grid=(4,),
+        out_shape=(
+            jax.ShapeDtypeStruct(image.shape, f32),
+            jax.ShapeDtypeStruct(field.shape, f32),
+        ),
+        in_specs=specs,
+        out_specs=specs,
+        name="hand_over",
+    )(image, field)
 
 
 def shards(wavefield, velocity, freq_index, owner):
@@ -606,7 +764,7 @@
             jax.ShapeDtypeStruct((2, ROWS, BAND), f32),
             jax.ShapeDtypeStruct((1, 2, ROWS, NX), f32),
         ),
-        in_specs=[smem, smem] + [vmem] * 8,
+        in_specs=[smem, smem] + [vmem] * 10,
         out_specs=(vmem, vmem),
         scratch_shapes=[
             pltpu.VMEM((TILES, CHUNK, 2 * LANES), f32),
@@ -638,14 +796,14 @@
             dma((1 + CHUNKS,)), dma((1 + CHUNKS, 32)), dma((1 + CHUNKS,)), dma((1 + CHUNKS,)), dma((CHUNKS,)),
             dma((6,)), dma((6,)), dma((2,)),
             dma((2, CHUNKS)), dma((2, CHUNKS)), dma((2, CHUNKS)),
-            dma((2,)), dma((2,)), dma((1,)),
+            dma((2,)), dma((2,)), dma((1,)), pltpu.SemaphoreType.REGULAR((2,)), dma((2, CHUNKS)), dma((32,)),
         ],
         compiler_params=pltpu.CompilerParams(
             collective_id=0, has_side_effects=True, vmem_limit_bytes=60 * 2**20
         ),
         name="migrate",
     )(freq_index, owner, wavefield, velocity[0], *tables())
-    return image, field
+    return hand_over(image, field)
 
 
 def solution(mesh):

time: 230 us -> 217 us (0.943)
  the two profiles are of different devices: /device:TPU:27 before, /device:TPU:8 now
where the time goes in v3:
time: 217 us
  Pallas kernels  216 us (100%)
    pallas_call x1, Pallas kernels, shards(): pl.pallas_call(kernel, out_shape=(jax.ShapeDtypeStruct((2, ROWS, BAND), f...  212 us

profile of v3, /device:TPU:8, one launch (start us, length us, event | category | flops | bytes accessed | tf_op | source)
XLA Modules:
  0.0 217.3 jit_solution(12796866044551886408)
XLA Ops:
  1.3 212.1 %migrate.1 = (f32[2,64,512]{2,1,0:T(8,128)}, f32[1,2,64,4096]{3,2,1,0:T(8,128)}) custom-call(s32[1]{0:T(128)S(6)} %copy.14.fidx_ref, s32[8]{0:T(128)} %owner_ref.1, f32[1,2,64,4096]{3,2,1,0:T(8,128)} %wave_ref.1, f32[64,4096]{1,0:T(8,128)} %bitcast.1, f32[32,128]{1,0:T(8,128)} %constant.16.clone.txc_ref, f32[32,128]{1,0:T(8,128)} %constant.17.clone.txs_ref, ...), custom_call_target="tpu_custom_call" | custom-call | tf_op jit(solution)/shard_map/migrate/pallas_call | solution.py:761
  213.4 3.9 %hand_over.1 = (f32[2,64,512]{2,1,0:T(8,128)}, f32[1,2,64,4096]{3,2,1,0:T(8,128)}) custom-call(f32[2,64,512]{2,1,0:T(8,128)} %get-tuple-element.4.image_in, f32[1,2,64,4096]{3,2,1,0:T(8,128)} %get-tuple-element.5.field_in), custom_call_target="tpu_custom_call" | custom-call | tf_op jit(solution)/shard_map/hand_over/pallas_call | solution.py:743

commit v4 on v3

--- a/solution.py
+++ b/solution.py
@@ -122,7 +122,7 @@
     rowbuf, sendx, sendy, recvy, recvx, relay, mid, hcos, hsin, tyc, tys,
     vrecv, vsel, vpart, vturn, slow, phc, phs, terms, imag, irecv, isum, iback, omega_out, omega_in,
     asend, arecv, aloc, rsend, rrecv, zsend, zrecv, rloc,
-    vsend, vrcv, vloc, isend, ircv, iloc, tsend, trecv, tloc, gate, csend, psend,
+    vsend, vrcv, vloc, isend, ircv, iloc, tsend, trecv, tloc, gate, gsend, grecv, csend, psend,
 ):
     f = lax.axis_index("freq")
     me = lax.axis_index("space")
@@ -536,16 +536,26 @@
 
     eighth = pl.ds(pl.multiple_of(z * PIECE, PIECE), PIECE)
 
+    def ring_copy(k):
+        offset = (2, -2, 1, -1, 1, -1, 2, -2)[k]
+        source = (0, 0, 0, 0, -2, 2, -2, 2)[k]
+        cols = (slice(0, NX // 2) if k == 6 else slice(NX // 2, NX)) if k >= 6 else slice(0, NX)
+        rows = pl.ds(pl.multiple_of((z + 8 + source) % 8 * PIECE, PIECE), PIECE)
+        part = slow.at[0, rows, cols]
+        return remote(part, part, gsend.at[k], grecv.at[k], along_z((8 + offset) % 8)[0])
+
     def velocity_along_z():
-        @pl.loop(1, 8)
-        def _(j):
-            remote(vturn, slow.at[0, eighth], vsend.at[4], vrcv.at[4], along_z(j)[0]).start()
-
         slow[0, eighth] = vturn[...]
-
-    def along_z_all():
-        part = slow.at[0, pl.ds(0, 7 * PIECE)]
-        return remote(part, part, vsend.at[4], vrcv.at[4], across_odd)
+        for k in range(4):
+            ring_copy(k).start()
+
+    def velocity_forward():
+        ring_copy(0).wait_recv()
+        ring_copy(1).wait_recv()
+        for k in range(4, 8):
+            ring_copy(k).start()
+        for k in range(2, 8):
+            ring_copy(k).wait_recv()
 
     def velocity_along_x():
         pair1.wait_recv()
@@ -634,7 +644,7 @@
         pl.semaphore_wait(gate.at[1], 1)
         velocity_spread()
 
-    along_z_all().wait_recv()
+    velocity_forward()
     make_phase(0, omega_in[0:1, 0:1])
     for ch in range(CHUNKS):
         a2a_wait_recv(recvx.at[0], ch, 0)
@@ -704,7 +714,8 @@
     velocity_all().wait_send()
     pair0.wait_send()
     pair1.wait_send()
-    along_z_all().wait_send()
+    for k in range(8):
+        ring_copy(k).wait_send()
     along_x_all().wait_send()
     for ch in range(CHUNKS):
         part = relay.at[1, :, chunk_rows(ch)]
@@ -796,7 +807,7 @@
             dma((1 + CHUNKS,)), dma((1 + CHUNKS, 32)), dma((1 + CHUNKS,)), dma((1 + CHUNKS,)), dma((CHUNKS,)),
             dma((6,)), dma((6,)), dma((2,)),
             dma((2, CHUNKS)), dma((2, CHUNKS)), dma((2, CHUNKS)),
-            dma((2,)), dma((2,)), dma((1,)), pltpu.SemaphoreType.REGULAR((2,)), dma((2, CHUNKS)), dma((32,)),
+            dma((2,)), dma((2,)), dma((1,)), pltpu.SemaphoreType.REGULAR((2,)), dma((8,)), dma((8,)), dma((2, CHUNKS)), dma((32,)),
         ],
         compiler_params=pltpu.CompilerParams(
             collective_id=0, has_side_effects=True, vmem_limit_bytes=60 * 2**20

time: 217 us -> 213 us (0.982)
  Pallas kernels: 216 us -> 211 us
    pallas_call x1, Pallas kernels: 212 us -> 207 us  [shards(): pl.pallas_call(kernel, out_shape=(jax.ShapeDtypeStruct((2, ROWS, BAND), f...]
where the time goes in v4:
time: 213 us; the launch traced here: 212 us
  Pallas kernels  211 us (99%)
    pallas_call x1, Pallas kernels, shards(): pl.pallas_call(kernel, out_shape=(jax.ShapeDtypeStruct((2, ROWS, BAND), f...  207 us

profile of v4, /device:TPU:8, one launch (start us, length us, event | category | flops | bytes accessed | tf_op | source)
XLA Modules:
  0.0 212.3 jit_solution(15072252865414451362)
XLA Ops:
  1.3 207.1 %migrate.1 = (f32[2,64,512]{2,1,0:T(8,128)}, f32[1,2,64,4096]{3,2,1,0:T(8,128)}) custom-call(s32[1]{0:T(128)S(6)} %copy.14.fidx_ref, s32[8]{0:T(128)} %owner_ref.1, f32[1,2,64,4096]{3,2,1,0:T(8,128)} %wave_ref.1, f32[64,4096]{1,0:T(8,128)} %bitcast.1, f32[32,128]{1,0:T(8,128)} %constant.16.clone.txc_ref, f32[32,128]{1,0:T(8,128)} %constant.17.clone.txs_ref, ...), custom_call_target="tpu_custom_call" | custom-call | tf_op jit(solution)/shard_map/migrate/pallas_call | solution.py:772
  208.4 3.9 %hand_over.1 = (f32[2,64,512]{2,1,0:T(8,128)}, f32[1,2,64,4096]{3,2,1,0:T(8,128)}) custom-call(f32[2,64,512]{2,1,0:T(8,128)} %get-tuple-element.4.image_in, f32[1,2,64,4096]{3,2,1,0:T(8,128)} %get-tuple-element.5.field_in), custom_call_target="tpu_custom_call" | custom-call | tf_op jit(solution)/shard_map/hand_over/pallas_call | solution.py:754

commit v5 on v4

--- a/solution.py
+++ b/solution.py
@@ -20,7 +20,7 @@
 CHUNKS = ROWS // CHUNK
 BAND = NX // FREQ
 PIECE = ROWS // FREQ
-AHEAD, BEHIND, WINDOW = 16, 16, 16
+AHEAD, BEHIND, WINDOW = 32, 32, 32
 
 cell_spacing = 25.0
 layer_thickness = 10.0
@@ -550,10 +550,10 @@
             ring_copy(k).start()
 
     def velocity_forward():
-        ring_copy(0).wait_recv()
-        ring_copy(1).wait_recv()
-        for k in range(4, 8):
-            ring_copy(k).start()
+        for k in range(2):
+            ring_copy(k).wait_recv()
+            ring_copy(4 + k).start()
+            ring_copy(6 + k).start()
         for k in range(2, 8):
             ring_copy(k).wait_recv()
 

time: 213 us -> 211 us (level)
    pallas_call x1, Pallas kernels: 207 us -> 205 us  [shards(): pl.pallas_call(kernel, out_shape=(jax.ShapeDtypeStruct((2, ROWS, BAND), f...]
where the time goes in v5:
time: 211 us; the launch traced here: 210 us
  Pallas kernels  209 us (99%)
    pallas_call x1, Pallas kernels, shards(): pl.pallas_call(kernel, out_shape=(jax.ShapeDtypeStruct((2, ROWS, BAND), f...  205 us

profile of v5, /device:TPU:8, one launch (start us, length us, event | category | flops | bytes accessed | tf_op | source)
XLA Modules:
  0.0 210.1 jit_solution(9262890803998883896)
XLA Ops:
  1.3 204.9 %migrate.1 = (f32[2,64,512]{2,1,0:T(8,128)}, f32[1,2,64,4096]{3,2,1,0:T(8,128)}) custom-call(s32[1]{0:T(128)S(6)} %copy.14.fidx_ref, s32[8]{0:T(128)} %owner_ref.1, f32[1,2,64,4096]{3,2,1,0:T(8,128)} %wave_ref.1, f32[64,4096]{1,0:T(8,128)} %bitcast.1, f32[32,128]{1,0:T(8,128)} %constant.16.clone.txc_ref, f32[32,128]{1,0:T(8,128)} %constant.17.clone.txs_ref, ...), custom_call_target="tpu_custom_call" | custom-call | tf_op jit(solution)/shard_map/migrate/pallas_call | solution.py:772
  206.2 3.9 %hand_over.1 = (f32[2,64,512]{2,1,0:T(8,128)}, f32[1,2,64,4096]{3,2,1,0:T(8,128)}) custom-call(f32[2,64,512]{2,1,0:T(8,128)} %get-tuple-element.4.image_in, f32[1,2,64,4096]{3,2,1,0:T(8,128)} %get-tuple-element.5.field_in), custom_call_target="tpu_custom_call" | custom-call | tf_op jit(solution)/shard_map/hand_over/pallas_call | solution.py:754
